TPU v7x, 128 devices: a whole 4x4x4 slice. The times are simulated.
128 devices in a mesh: seq: 2 (over y_hi), dp: 64 (over y_lo, z, x, core).
Axes of the slice: x: 4, y: 4 (y_hi: 2, y_lo: 2; y = y_hi * 2 + y_lo), z: 4, core: 2. Of those that a mesh axis runs over, the one named last changes fastest.
Arguments:
- tokens: bfloat16 [16384, 1024], P(('seq', 'dp')), may hold values from -6 to 6
- ln1_gain: bfloat16 [1024], P('dp'), may hold values from 0.099609375 to 1.8984375
- ln1_bias: bfloat16 [1024], P('dp'), may hold values from -4 to 4
- ln2_gain: bfloat16 [1024], P('dp'), may hold values from 0.099609375 to 1.8984375
- ln2_bias: bfloat16 [1024], P('dp'), may hold values from -4 to 4
- qkv_weight: bfloat16 [1024, 3072], P('dp'), may hold values from -0.1875 to 0.1875
- qkv_bias: bfloat16 [3072], P('dp'), may hold values from -4 to 4
- dense_weight: bfloat16 [1024, 1024], P('dp'), may hold values from -1.5 to 1.5
- dense_bias: bfloat16 [1024], P('dp'), may hold values from -4 to 4
- fc_in_weight: bfloat16 [1024, 4096], P('dp'), may hold values from -0.1875 to 0.1875
- fc_in_bias: bfloat16 [4096], P('dp'), may hold values from -4 to 4
- fc_out_weight: bfloat16 [4096, 1024], P('dp'), may hold values from -0.09375 to 0.09375
- fc_out_bias: bfloat16 [1024], P('dp'), may hold values from -4 to 4
- out_grad: bfloat16 [16384, 1024], P(('seq', 'dp')), may hold values from -6 to 6
Outputs:
- mixed: bfloat16 [16384, 1024], P(('seq', 'dp'))
- tokens_grad: float32 [16384, 1024], P(('seq', 'dp'))
- ln1_gain_grad: float32 [1024], P('dp')
- ln1_bias_grad: float32 [1024], P('dp')
- ln2_gain_grad: float32 [1024], P('dp')
- ln2_bias_grad: float32 [1024], P('dp')
- qkv_weight_grad: float32 [1024, 3072], P('dp')
- qkv_bias_grad: float32 [3072], P('dp')
- dense_weight_grad: float32 [1024, 1024], P('dp')
- dense_bias_grad: float32 [1024], P('dp')
- fc_in_weight_grad: float32 [1024, 4096], P('dp')
- fc_in_bias_grad: float32 [4096], P('dp')
- fc_out_weight_grad: float32 [4096, 1024], P('dp')
- fc_out_bias_grad: float32 [1024], P('dp')
All inputs are finite; a program needn't handle non-finite values.
Results may differ from a plain program's by a relative error of at most 0.011.
Values may be sent and summed in bfloat16 or wider, within the bound.
No kernel may reach another device: no remote copies, remote signals or barrier semaphores. Data moves between devices by JAX's collectives and lax.ppermute only.
A program may use at most 192 MiB of HBM per device.

v0:
```python
import jax
import jax.numpy as jnp
from jax import lax
from jax.experimental import pallas as pl
from jax.experimental.pallas import tpu as pltpu
from jax.sharding import Mesh
from jax.sharding import PartitionSpec as P

HEADS = 16
HEAD_DIM = 64
ROT = 16
WIDTH = 1024
FF = 4096
TOK = 128
F32 = jnp.float32
BF16 = jnp.bfloat16
EPSILON = 1e-05
AXES = ("s", "yl", "z", "x", "c")
GROUP = ("s", "yl", "c")
OWNERS = ("yl", "z", "x", "c")
QKV = 384
HID = 512
COLS = QKV + HID
COUNTS = (1, 1, 1, 1, 1, 1, 3, 4)
VMEM_LIMIT = 60 * 1024 * 1024


def swap_piece(values):
    return lax.ppermute(values, "s", [(0, 1), (1, 0)])


def spread(blocks, axes):
    return lax.all_to_all(blocks, axes, split_axis=0, concat_axis=0, tiled=True)


def after(values, first):
    return lax.optimization_barrier((values, first))[0]


def smem():
    return pl.BlockSpec(memory_space=pltpu.SMEM)


def vmem():
    return pl.BlockSpec(memory_space=pltpu.VMEM)


def call(body, out_shape, operands, flops=0, size=1 << 10):
    return pl.pallas_call(
        body,
        out_shape=out_shape,
        in_specs=[smem()] + [vmem()] * (len(operands) - 1),
        out_specs=jax.tree.map(lambda _: vmem(), out_shape),
        compiler_params=pltpu.CompilerParams(vmem_limit_bytes=VMEM_LIMIT),
        cost_estimate=pl.CostEstimate(flops=flops, bytes_accessed=size, transcendentals=0),
    )(*operands)


def per_owner(out, yl, c, block):
    for place in range(16):
        out[(yl * 16 + place) * 2 + c] = block


def columns_of(vector, count):
    size = 16 * count
    wide = jnp.broadcast_to(vector[...].astype(F32)[None, :], (16, size))
    row = lax.broadcasted_iota(jnp.int32, (16, size), 0)
    lane = lax.broadcasted_iota(jnp.int32, (16, size), 1)
    return [
        jnp.sum(jnp.where(lane == row * count + i, wide, 0.0), axis=1, keepdims=True) for i in range(count)
    ]


def pack_body(at, *refs):
    vectors, out, copies, done = refs[:10], refs[10], refs[11:21], refs[21]
    qkv, fc_in = copies[8:]
    started = [pltpu.make_async_copy(a, b, done.at[i]) for i, (a, b) in enumerate(zip(vectors, copies))]
    for copy in started:
        copy.start()
    for copy in started:
        copy.wait()
    lane = lax.broadcasted_iota(jnp.int32, (16, 128), 1)
    small = jnp.zeros((16, 128), F32)
    columns = []
    for vector, count in zip(copies, COUNTS):
        columns += columns_of(vector, count)
    for index, column in enumerate(columns):
        small = jnp.where(lane == index, column, small)
    small = small.astype(BF16)
    for yl in range(2):
        for c in range(2):
            parts = []
            for part in range(3):
                first = pl.multiple_of(part * WIDTH + at[0] * 512 + (yl * 2 + c) * 128, 128)
                parts.append(qkv[:, pl.ds(first, 128)])
            first = pl.multiple_of(at[0] * 2048 + (yl * 2 + c) * HID, HID)
            parts += [small, fc_in[:, pl.ds(first, HID)]]
            per_owner(out, yl, c, jnp.concatenate(parts, axis=1))


def pack(at, qkv_weight, fc_in_weight, vectors):
    anywhere = pl.BlockSpec(memory_space=pltpu.HBM)
    return pl.pallas_call(
        pack_body,
        out_shape=jax.ShapeDtypeStruct((64, 16, WIDTH), BF16),
        in_specs=[smem()] + [anywhere] * 10,
        out_specs=vmem(),
        scratch_shapes=[pltpu.VMEM((16 * count,), BF16) for count in COUNTS]
        + [pltpu.VMEM((16, 3 * WIDTH), BF16), pltpu.VMEM((16, FF), BF16), pltpu.SemaphoreType.DMA((10,))],
        compiler_params=pltpu.CompilerParams(vmem_limit_bytes=VMEM_LIMIT),
        cost_estimate=cost(0, 0),
    )(at, *vectors, qkv_weight, fc_in_weight)


def norm_stats(tokens):
    inputs = tokens[...].astype(F32)
    centered = inputs - jnp.mean(inputs, axis=1, keepdims=True)
    inverse = lax.rsqrt(jnp.mean(centered * centered, axis=1, keepdims=True) + EPSILON)
    return inputs, centered * inverse, inverse


def norm_body(at, tokens, out):
    out[...] = norm_stats(tokens)[1].astype(BF16)


def outputs_body(at, tokens, out_grad, norm_grad, mixed_sum, columns, mixed, tokens_grad):
    inputs, normed, inverse = norm_stats(tokens)
    sel = lax.broadcasted_iota(jnp.int32, (8, 128), 1)
    sel = jnp.where((sel == 4) | (sel == 5), 1.0, 0.0).astype(BF16)
    bias = nt_dot(sel, columns[:, QKV:512])[0:1]
    mixed[...] = (inputs + mixed_sum[...].astype(F32) + bias).astype(BF16)
    grad = norm_grad[...].astype(F32)
    mean_grad = jnp.mean(grad, axis=1, keepdims=True)
    mean_dot = jnp.mean(grad * normed, axis=1, keepdims=True)
    tokens_grad[...] = out_grad[...].astype(F32) + inverse * (grad - mean_grad - normed * mean_dot)


def tail_in_body(blocks, ahead, out):
    for place in range(16):
        k, lane = place // 2, (place % 2) * 512
        out[k * 16 : k * 16 + 16, lane : lane + 512] = blocks[place, 0:16, :]
        out[128 + k * 64 : 192 + k * 64, lane : lane + 512] = blocks[place, 16:80, :]


def owner_body(at, near, far, qkv_out, in_out, g1, b1, g2, b2, bias, qb, fb):
    small = jnp.zeros((16, 128), F32)
    for block, mine in ((near, at[0]), (far, 1 - at[0])):
        for j in range(4):
            for part in range(3):
                first = pl.multiple_of(part * WIDTH + mine * 512 + j * 128, 128)
                qkv_out[:, pl.ds(first, 128)] = block[j, :, part * 128 : part * 128 + 128].astype(F32)
            small = small + block[j, :, QKV:512].astype(F32)
            in_out[:, pl.ds(pl.multiple_of(mine * 2048 + j * HID, HID), HID)] = block[j, :, 512:].astype(F32)
    lane = 0
    for vector, count in ((g1, 1), (b1, 1), (g2, 1), (b2, 1), (bias, 1), (None, 1), (qb, 3), (fb, 4)):
        if vector is not None:
            size = 16 * count
            row = lax.broadcasted_iota(jnp.int32, (16, size), 0)
            place = lax.broadcasted_iota(jnp.int32, (16, size), 1)
            total = jnp.zeros((16, size), F32)
            for i in range(count):
                total = jnp.where(place == row * count + i, small[:, lane + i : lane + i + 1], total)
            vector[...] = jnp.sum(total, axis=0)
        lane += count


def nt_dot(left, right):
    return lax.dot_general(left, right, (((1,), (1,)), ((), ())), preferred_element_type=F32)


def tn_dot(left, right):
    return lax.dot_general(left, right, (((0,), (0,)), ((), ())), preferred_element_type=F32)


def dot(left, right):
    return jnp.dot(left, right, preferred_element_type=F32)


def bias_places(rank, shape, dim):
    column = lax.broadcasted_iota(jnp.int32, shape, dim)
    part, within = lax.shift_right_logical(column, 7), lax.bitwise_and(column, 127)
    q_column = part * WIDTH + rank * 128 + within
    h_column = rank * HID + column - QKV
    q_row = lax.div(q_column, 3)
    is_q = column < QKV
    row = jnp.where(is_q, q_row, lax.shift_right_logical(h_column, 2))
    lane = jnp.where(is_q, 6 + q_column - 3 * q_row, 9 + lax.bitwise_and(h_column, 3))
    return row, lane


def turn(values, cosine, low, high, sign):
    back = pltpu.roll(values, 128 - 8, 1)
    ahead = pltpu.roll(values, 8, 1)
    return values * cosine + sign * (back * low + ahead * high)


def causal():
    row = lax.broadcasted_iota(jnp.int32, (256, 256), 0)
    return row >= lax.broadcasted_iota(jnp.int32, (256, 256), 1)


def forward_body(at, xh, columns, cos, sin_low, sin_high, rotated, sums, both, slope, scaled, bias):
    rank = at[5]

    @pl.when(pl.program_id(0) == 0)
    def _():
        params = columns[:, QKV:512]
        weights = jnp.concatenate([columns[:, :QKV], columns[:, 512:]], axis=1)
        row, lane = bias_places(rank, (WIDTH, COLS), 1)
        hot = (lax.broadcasted_iota(jnp.int32, (WIDTH, COLS), 0) == row).astype(F32).astype(BF16)
        row, lane = bias_places(rank, (128, COLS), 1)
        sub = lax.broadcasted_iota(jnp.int32, (128, COLS), 0)
        column = lax.broadcasted_iota(jnp.int32, (128, COLS), 1)
        own = jnp.where(sub == lane, tn_dot(params, hot), 0.0)
        shifted = jnp.where(sub == jnp.where(column < QKV, 1, 3), tn_dot(params, weights), 0.0)
        bias[...] = jnp.sum(own + shifted, axis=0, keepdims=True)
        gains = params.astype(F32)
        scaled[:, :QKV] = (weights[:, :QKV].astype(F32) * gains[:, 0:1]).astype(BF16)
        scaled[:, QKV:] = (weights[:, QKV:].astype(F32) * gains[:, 2:3]).astype(BF16)

    tokens = xh[...].reshape(256, WIDTH)
    proj = dot(tokens, scaled[:, :QKV]) + bias[:, :QKV]
    table = cos[...], sin_low[...], sin_high[...]
    queries = turn(proj[:, 0:128], *table, 1.0).astype(BF16)
    keys = turn(proj[:, 128:256], *table, 1.0).astype(BF16)
    values = proj[:, 256:384].astype(BF16)
    rotated[...] = jnp.concatenate([queries, keys, values], axis=1).reshape(rotated.shape)
    allowed = causal()
    outs, logs = [], []
    for h in range(2):
        lanes = slice(h * HEAD_DIM, (h + 1) * HEAD_DIM)
        scores = jnp.where(allowed, nt_dot(queries[:, lanes], keys[:, lanes]) * HEAD_DIM ** (-0.5), -1e30)
        peak = jnp.max(scores, axis=1, keepdims=True)
        weights = jnp.exp(scores - peak)
        norm = jnp.sum(weights, axis=1, keepdims=True)
        outs.append(dot((weights / norm).astype(BF16), values[:, lanes]))
        logs.append(jnp.broadcast_to(peak + jnp.log(norm), (256, HEAD_DIM)))
    sums[...] = jnp.concatenate(logs, axis=1).reshape(sums.shape)
    attended = jnp.concatenate(outs, axis=1).astype(BF16)
    hidden = dot(tokens, scaled[:, QKV:]) + bias[:, QKV:]
    cdf = 0.5 * (1.0 + lax.erf(hidden * (0.5**0.5)))
    both[...] = jnp.concatenate([attended, (hidden * cdf).astype(BF16)], axis=1).reshape(both.shape)
    slope[...] = (cdf + hidden * jnp.exp(-0.5 * hidden * hidden) * 0.3989422804014327).reshape(slope.shape)


def token_spec(lanes):
    return pl.BlockSpec((2, 1, TOK, lanes), lambda i: (0, i, 0, 0))


def token_shape(lanes, dtype):
    return jax.ShapeDtypeStruct((2, 4, TOK, lanes), dtype)


def whole(rows, lanes):
    return pl.BlockSpec((rows, lanes), lambda i: (0, 0))


def cost(flops, size):
    return pl.CostEstimate(flops=flops >> 10, bytes_accessed=size >> 10, transcendentals=0)


def forward(at, xh, columns, tables):
    table = whole(256, 128)
    return pl.pallas_call(
        forward_body,
        grid=(4,),
        out_shape=(
            token_shape(QKV, BF16),
            token_shape(128, F32),
            token_shape(128 + HID, BF16),
            token_shape(HID, F32),
            jax.ShapeDtypeStruct((WIDTH, COLS), BF16),
        ),
        in_specs=[smem(), token_spec(WIDTH), whole(WIDTH, WIDTH), table, table, table],
        out_specs=(
            token_spec(QKV),
            token_spec(128),
            token_spec(128 + HID),
            token_spec(HID),
            whole(WIDTH, COLS),
        ),
        scratch_shapes=[pltpu.VMEM((1, COLS), F32)],
        compiler_params=pltpu.CompilerParams(vmem_limit_bytes=VMEM_LIMIT),
        cost_estimate=cost(4 << 30, 8 << 20),
    )(at, xh, columns, *tables)


def mixed_body(both, tail, out):
    features = both[...].reshape(256, 128 + HID)
    out[...] = dot(features, tail[...]).astype(BF16).reshape(out.shape)


def mixed_of(both, tail):
    return pl.pallas_call(
        mixed_body,
        grid=(4,),
        out_shape=token_shape(WIDTH, BF16),
        in_specs=[token_spec(128 + HID), whole(640, WIDTH)],
        out_specs=token_spec(WIDTH),
        compiler_params=pltpu.CompilerParams(vmem_limit_bytes=VMEM_LIMIT),
        cost_estimate=cost(2 << 30, 6 << 20),
    )(both, tail)


def sequence_step(rotated, sums, slope, cot, tail, scaled, cos, sin_low, sin_high, grads, norm):
    cotangent = cot[...].reshape(256, WIDTH)
    table = cos[...], sin_low[...], sin_high[...]
    packed, logs = rotated[...].reshape(256, QKV), sums[...].reshape(256, 128)
    grad = nt_dot(cotangent, tail[:128]).astype(BF16)
    dhid = (nt_dot(cotangent, tail[128:]) * slope[...].reshape(256, HID)).astype(BF16)
    allowed = causal()
    dqs, dks, dvs = [], [], []
    scale = HEAD_DIM ** (-0.5)
    for h in range(2):
        q, k, v = (packed[:, i * 128 + h * HEAD_DIM : i * 128 + (h + 1) * HEAD_DIM] for i in range(3))
        g = grad[:, h * HEAD_DIM : (h + 1) * HEAD_DIM]
        scores = nt_dot(q, k) * scale - logs[:, h * HEAD_DIM : h * HEAD_DIM + 1]
        probs = jnp.exp(jnp.where(allowed, scores, -1e30))
        dprobs = nt_dot(g, v)
        inner = jnp.sum(probs * dprobs, axis=1, keepdims=True)
        ds = (probs * (dprobs - inner)).astype(BF16)
        dqs.append(dot(ds, k) * scale)
        dks.append(tn_dot(ds, q) * scale)
        dvs.append(tn_dot(probs.astype(BF16), g))
    dq = turn(jnp.concatenate(dqs, axis=1).astype(BF16).astype(F32), *table, -1.0)
    dk = turn(jnp.concatenate(dks, axis=1).astype(BF16).astype(F32), *table, -1.0)
    dv = jnp.concatenate(dvs, axis=1)
    back = jnp.concatenate([dq.astype(BF16), dk.astype(BF16), dv.astype(BF16), dhid], axis=1)
    grads[:, pl.program_id(0)] = back.reshape(2, TOK, COLS)
    norm[...] = nt_dot(back, scaled[...]).astype(BF16).reshape(norm.shape)


def columns_step(at, xh, columns, total, out, stored, sums, spots):
    rank, block = at[5], pl.program_id(0) - 4
    grads = stored[...].reshape(WIDTH, COLS)

    @pl.when(block == 0)
    def _():
        sums[...] = dot(jnp.ones((8, WIDTH), BF16), grads)
        row, lane = bias_places(rank, (128, COLS), 1)
        sub = lax.broadcasted_iota(jnp.int32, (128, COLS), 0)
        spots[...] = jnp.where(sub == lane, sums[0:1, :], 0.0).astype(BF16)

    product = tn_dot(xh[...], grads)
    total_cols = sums[0:1, :]
    params = columns[:, QKV:512].astype(F32)
    weights = jnp.concatenate([columns[:, :QKV], columns[:, 512:]], axis=1).astype(F32)
    row, lane = bias_places(rank, (256, COLS), 1)
    here = block * 256 + lax.broadcasted_iota(jnp.int32, (256, COLS), 0)
    hot = (here == row).astype(F32).astype(BF16)
    small = nt_dot(hot, spots[...])
    lane = lax.broadcasted_iota(jnp.int32, (256, 128), 1)
    mirror = lax.broadcasted_iota(jnp.int32, (256, 256), 0) == lax.broadcasted_iota(jnp.int32, (256, 256), 1)
    mine = jnp.sum(jnp.where(mirror, total[0:1, :], 0.0), axis=1, keepdims=True)
    small = jnp.where((lane == 4) & (rank == 0), mine, small)
    for first, last, index in ((0, QKV, 0), (QKV, COLS, 2)):
        w, g, t = weights[:, first:last], product[:, first:last], total_cols[:, first:last]
        small = jnp.where(lane == index, jnp.sum(w * g, axis=1, keepdims=True), small)
        small = jnp.where(lane == index + 1, jnp.sum(w * t, axis=1, keepdims=True), small)
        change = (params[:, index : index + 1] * g + params[:, index + 1 : index + 2] * t).astype(BF16)
        start = 0 if first == 0 else 512
        out[:, start : start + last - first] = change
    out[:, QKV:512] = small.astype(BF16)


def backward_body(
    at, rotated, sums, slope, cot, tail, scaled, cos, sin_low, sin_high, xh, columns, total, one, two, norm, out, grads, cols, spots
):
    @pl.when(pl.program_id(0) < 4)
    def _():
        sequence_step(rotated, sums, slope, cot, tail, scaled, cos, sin_low, sin_high, grads, norm)

    @pl.when(pl.program_id(0) >= 4)
    def _():
        columns_step(at, xh, columns, total, out, grads, cols, spots)


def backward(at, rotated, sums, slope, cot, tail, scaled, tables, xh, columns, total, one, two):
    def tokens(lanes):
        return pl.BlockSpec((2, 1, TOK, lanes), lambda i: (0, jnp.minimum(i, 3), 0, 0))

    def later(i):
        return jnp.maximum(i - 4, 0)

    table = whole(256, 128)
    anywhere = pl.BlockSpec(memory_space=pl.ANY)
    return pl.pallas_call(
        backward_body,
        grid=(8,),
        out_shape=(token_shape(WIDTH, BF16), jax.ShapeDtypeStruct((WIDTH, WIDTH), BF16)),
        in_specs=[
            smem(),
            tokens(QKV),
            tokens(128),
            tokens(HID),
            tokens(WIDTH),
            whole(640, WIDTH),
            whole(WIDTH, COLS),
            table,
            table,
            table,
            pl.BlockSpec((WIDTH, 256), lambda i: (0, later(i))),
            pl.BlockSpec((256, WIDTH), lambda i: (later(i), 0)),
            pl.BlockSpec((8, 256), lambda i: (0, later(i))),
            anywhere,
            anywhere,
        ],
        out_specs=(tokens(WIDTH), pl.BlockSpec((256, WIDTH), lambda i: (later(i), 0))),
        scratch_shapes=[
            pltpu.VMEM((2, 4, TOK, COLS), BF16),
            pltpu.VMEM((8, COLS), F32),
            pltpu.VMEM((128, COLS), BF16),
        ],
        compiler_params=pltpu.CompilerParams(vmem_limit_bytes=VMEM_LIMIT),
        cost_estimate=cost(6 << 30, 16 << 20),
    )(at, rotated, sums, slope, cot, tail, scaled, *tables, xh, columns, total, one, two)


def tail_grad_body(both, cot, out, total):
    for half in range(2):
        product = tn_dot(both[...], cot[:, half * 512 : half * 512 + 512]).astype(BF16)
        for k in range(8):
            out[2 * k + half, 0:16, :] = product[k * 16 : k * 16 + 16]
            out[2 * k + half, 16:80, :] = product[128 + k * 64 : 192 + k * 64]
    total[...] = dot(jnp.ones((8, WIDTH), BF16), cot[...])


def tail_grad_of(both, cot):
    return pl.pallas_call(
        tail_grad_body,
        out_shape=(jax.ShapeDtypeStruct((16, 80, 512), BF16), jax.ShapeDtypeStruct((8, WIDTH), F32)),
        in_specs=[vmem(), vmem()],
        out_specs=(vmem(), vmem()),
        compiler_params=pltpu.CompilerParams(vmem_limit_bytes=VMEM_LIMIT),
        cost_estimate=cost(2 << 30, 6 << 20),
    )(both, cot)


def tail_in(blocks, ahead):
    return pl.pallas_call(
        tail_in_body,
        out_shape=jax.ShapeDtypeStruct((640, WIDTH), BF16),
        in_specs=[vmem(), pl.BlockSpec(memory_space=pl.ANY)],
        out_specs=vmem(),
        compiler_params=pltpu.CompilerParams(vmem_limit_bytes=VMEM_LIMIT),
        cost_estimate=cost(0, 0),
    )(blocks, ahead)


def rotary_tables():
    position = jnp.arange(256).astype(F32)[:, None]
    lane = jnp.arange(128) % HEAD_DIM
    halves = (lane % (ROT // 2)).astype(F32)
    frequency = jnp.power(10000.0, -2.0 * halves / ROT)[None, :]
    angle = position * frequency
    cosine, sine = jnp.cos(angle), jnp.sin(angle)
    lane = lane[None, :]
    return (
        jnp.where(lane < ROT, cosine, 1.0),
        jnp.where(lane < ROT // 2, -sine, 0.0),
        jnp.where((lane >= ROT // 2) & (lane < ROT), sine, 0.0),
    )


def gather_tokens(block):
    return lax.all_gather(block, GROUP, axis=0, tiled=True)


def scatter_tokens(partial):
    return lax.psum_scatter(partial, GROUP, scatter_dimension=0, tiled=True)


def tail_routes():
    straight, crossed = [], []
    for s in range(2):
        for dp in range(64):
            rank, place = dp // 8, 2 * (dp % 8) + s
            target_dp = (((rank >> 1) & 1) * 16 + place) * 2 + (rank & 1)
            target = (rank >> 2) * 64 + target_dp
            straight.append((s * 64 + dp, target))
            crossed.append(((1 - s) * 64 + dp, target))
    return straight, crossed


def local(
    tokens,
    ln1_gain,
    ln1_bias,
    ln2_gain,
    ln2_bias,
    qkv_weight,
    qkv_bias,
    dense_weight,
    dense_bias,
    fc_in_weight,
    fc_in_bias,
    fc_out_weight,
    fc_out_bias,
    out_grad,
):
    s, yl, z, x, c = (lax.axis_index(a) for a in AXES)
    rank = s * 4 + yl * 2 + c
    at = jnp.stack([s, yl, z, x, c, rank]).astype(jnp.int32)
    straight, crossed = tail_routes()
    shape = jax.ShapeDtypeStruct

    vectors = (ln1_gain, ln1_bias, ln2_gain, ln2_bias, dense_bias, fc_out_bias, qkv_bias, fc_in_bias)
    sent = pack(at, qkv_weight, fc_in_weight, vectors)
    columns_in = spread(sent, OWNERS).reshape(WIDTH, 1024)
    tail = jnp.concatenate([dense_weight, fc_out_weight], axis=0)
    tail = lax.dynamic_slice_in_dim(tail, s * 512, 512, axis=1)
    tail = lax.ppermute(tail, AXES, straight)
    tail = spread(jnp.broadcast_to(after(tail, columns_in), (16, 80, 512)), ("z", "x"))

    own_xh = call(norm_body, shape((TOK, WIDTH), BF16), (at, tokens))
    xh = gather_tokens(own_xh)
    cot = gather_tokens(after(out_grad, own_xh))

    xh_tokens, cot_tokens = xh.reshape(2, 4, TOK, WIDTH), cot.reshape(2, 4, TOK, WIDTH)
    tables = rotary_tables()
    rotated, sums, both, slope, scaled = forward(at, xh_tokens, columns_in, tables)
    tail = tail_in(tail, slope)
    tail_grad, total = tail_grad_of(both.reshape(WIDTH, 640), cot)
    tail_parts = spread(tail_grad, ("z", "x"))
    mixed_part = mixed_of(both, tail)
    mixed_sum = scatter_tokens(mixed_part.reshape(WIDTH, WIDTH))
    norm_part, columns_grad = backward(
        at, rotated, sums, slope, cot_tokens, tail, scaled, tables, xh, columns_in, total, tail_grad, mixed_part
    )
    norm_part, columns_grad = after((norm_part, columns_grad), (mixed_sum, tail_parts))
    norm_grad = scatter_tokens(norm_part.reshape(WIDTH, WIDTH))
    tail_sum = jnp.sum(tail_parts.astype(F32), axis=0).astype(BF16)
    parts = spread(columns_grad.reshape(64, 16, 1024), OWNERS).reshape(2, 16, 2, 16, 1024)
    near = jnp.sum(parts.astype(F32), axis=1).reshape(4, 16, 1024)
    far = swap_piece(near.astype(BF16))
    vector = shape((16,), F32)
    qkv_grad, fc_in_grad, g1_grad, b1_grad, g2_grad, b2_grad, bias_grad, qb_grad, fb_grad = call(
        owner_body,
        (shape((16, 3 * WIDTH), F32), shape((16, FF), F32))
        + (vector,) * 5
        + (shape((48,), F32), shape((64,), F32)),
        (at, near, far),
    )
    mine = lax.ppermute(tail_sum, AXES, [(b, a) for a, b in straight])
    other = lax.ppermute(tail_sum, AXES, [(b, a) for a, b in crossed])
    is_first = s == 0
    left, right = jnp.where(is_first, mine, other), jnp.where(is_first, other, mine)
    tail_full = jnp.concatenate([left, right], axis=1).astype(F32)

    mixed, tokens_grad = call(
        outputs_body,
        (shape((TOK, WIDTH), BF16), shape((TOK, WIDTH), F32)),
        (at, tokens, out_grad, norm_grad, mixed_sum, columns_in),
    )
    return (
        mixed,
        tokens_grad,
        g1_grad,
        b1_grad,
        g2_grad,
        b2_grad,
        qkv_grad,
        qb_grad,
        tail_full[:16],
        bias_grad,
        fc_in_grad,
        fb_grad,
        tail_full[16:],
        bias_grad,
    )


def solution(mesh):
    grid = Mesh(mesh.devices.reshape(2, 2, 4, 4, 2), AXES)
    rows = P(AXES, None)
    vector = P(AXES[1:])
    matrix = P(AXES[1:], None)
    in_specs = (
        rows,
        vector,
        vector,
        vector,
        vector,
        matrix,
        vector,
        matrix,
        vector,
        matrix,
        vector,
        matrix,
        vector,
        rows,
    )
    out_specs = (
        rows,
        rows,
        vector,
        vector,
        vector,
        vector,
        matrix,
        vector,
        matrix,
        vector,
        matrix,
        vector,
        matrix,
        vector,
    )
    return jax.shard_map(local, mesh=grid, in_specs=in_specs, out_specs=out_specs, check_vma=False)
```

profile of v0, /device:TPU:1, one launch (start us, length us, event | category | flops | bytes accessed | tf_op | source)
XLA Modules:
  0.0 202.6 jit_solution(2633292593254169309)
XLA Ops:
  7.2 0.0 all-gather.3.cloned.1.call-start
  7.2 0.6 stack.27.at
  7.8 1.9 shard_map.245
  9.7 0.0 all-gather.3.cloned.1.call-update
  9.8 0.0 all-gather.5.cloned.1.call-start
  9.8 0.7 all-gather.5.cloned.1.call-update
  10.5 3.4 %shard_map.246 = bf16[64,16,1024]{2,1,0:T(8,128)(2,1)} custom-call(s32[6]{0:T(128)} %stack.27.at, bf16[16]{0:T(256)(128)(2,1)} %refs_0_.1, bf16[16]{0:T(256)(128)(2,1)} %refs_1_.1, bf16[16]{0:T(256)(128)(2,1)} %refs_2_.1, bf16[16]{0:T(256)(128)(2,1)} %refs_3_.1, bf16[16]{0:T(256)(128)(2,1)} %refs_4_.1, bf16[16]{0:T(256)(128)(2,1)} %refs_5_.1, ...), custom_call_target="tpu_custom_call" | custom-call | tf_op jit(solution)/shard_map/pallas_call | solution.py:103
  13.9 0.0 copy-start.4
  13.9 0.0 copy-start.5
  13.9 11.0 %all-to-all-start = ((bf16[64,16,1024]{2,1,0:T(8,128)(2,1)}), bf16[64,16,1024]{2,1,0:T(8,128)(2,1)S(1)}, u32[]{:S(2)}, u32[]{:S(2)}) async-start(bf16[64,16,1024]{2,1,0:T(8,128)(2,1)} %shard_map.246), calls=%async_computation | async-start | bytes 4194304 | tf_op jit(solution)/shard_map/all_to_all | solution.py:33
  25.0 0.0 copy-done.4
  25.0 0.0 copy-done.5
  25.0 5.0 %collective-permute-start = (bf16[80,512]{1,0:T(8,128)(2,1)S(1)}, bf16[80,512]{1,0:T(8,128)(2,1)S(1)}, u32[]{:S(2)}, u32[]{:S(2)}) collective-permute-start(bf16[80,512]{1,0:T(8,128)(2,1)S(1)} %fusion.5), channel_id=1, source_target_pairs={{0,0},{1,4},{2,8},{3,12},{4,16},{5,20},{6,24},{7,28},{8,1},{9,5},{... | collective-permute-start | bytes 245768 | tf_op jit(solution)/shard_map/ppermute | solution.py:512
  30.0 18.6 %collective-permute-done = bf16[80,512]{1,0:T(8,128)(2,1)S(1)} collective-permute-done((bf16[80,512]{1,0:T(8,128)(2,1)S(1)}, bf16[80,512]{1,0:T(8,128)(2,1)S(1)}, u32[]{:S(2)}, u32[]{:S(2)}) %collective-permute-start) | collective-permute-done | bytes 81952 | tf_op jit(solution)/shard_map/ppermute | solution.py:512
  48.6 10.8 %all-to-all-done = bf16[64,16,1024]{2,1,0:T(8,128)(2,1)S(1)} async-done(((bf16[64,16,1024]{2,1,0:T(8,128)(2,1)}), bf16[64,16,1024]{2,1,0:T(8,128)(2,1)S(1)}, u32[]{:S(2)}, u32[]{:S(2)}) %all-to-all-start) | async-done | bytes 2097184 | tf_op jit(solution)/shard_map/all_to_all | solution.py:33
  59.5 0.0 copy-start
  59.5 1.3 broadcast_in_dim.43
  60.8 8.9 %all-to-all-start.1 = ((bf16[16,80,512]{2,1,0:T(8,128)(2,1)}), bf16[16,80,512]{2,1,0:T(8,128)(2,1)S(1)}, u32[]{:S(2)}, u32[]{:S(2)}) async-start(bf16[16,80,512]{2,1,0:T(8,128)(2,1)} %broadcast_in_dim.43), calls=%async_computation.1 | async-start | bytes 2621440 | tf_op jit(solution)/shard_map/all_to_all | solution.py:33
  69.7 0.0 reduce-scatter.3.cloned.1.call-start
  69.8 1.3 fusion
  71.1 0.0 copy-done
  71.1 0.0 all-gather.3.cloned.1.call-done.xh
  71.1 10.7 %shard_map.247 = (bf16[2,4,128,384]{3,2,1,0:T(8,128)(2,1)}, f32[2,4,128,128]{3,2,1,0:T(8,128)}, bf16[2,4,128,640]{3,2,1,0:T(8,128)(2,1)}, f32[2,4,128,512]{3,2,1,0:T(8,128)}, bf16[1024,896]{1,0:T(8,128)(2,1)}) custom-call(s32[6]{0:T(128)} %stack.27.at, bf16[2,4,128,1024]{3,2,1,0:T(8,128)(2,1)} %bitcast.21, bf16[1024,1024]{1,0:T(8,128)(2,1)} %bitcast.17, ...), custom_call_target="tpu_custom_call" | custom-call | flops 4194304 | bytes 8192 | tf_op jit(solution)/shard_map/pallas_call | solution.py:264
  81.8 10.9 %all-to-all-done.1.blocks = bf16[16,80,512]{2,1,0:T(8,128)(2,1)S(1)} async-done(((bf16[16,80,512]{2,1,0:T(8,128)(2,1)}), bf16[16,80,512]{2,1,0:T(8,128)(2,1)S(1)}, u32[]{:S(2)}, u32[]{:S(2)}) %all-to-all-start.1) | async-done | bytes 1310752 | tf_op jit(solution)/shard_map/all_to_all | solution.py:33
  92.7 0.0 copy-start.1
  92.7 1.1 copy-done.1
  93.8 2.5 %shard_map.248.tail = bf16[640,1024]{1,0:T(8,128)(2,1)} custom-call(bf16[16,80,512]{2,1,0:T(8,128)(2,1)} %copy-done.1, f32[2,4,128,512]{3,2,1,0:T(8,128)} %get-tuple-element.40.ahead.slope), custom_call_target="tpu_custom_call" | custom-call | tf_op jit(solution)/shard_map/pallas_call | solution.py:440
  96.3 5.2 %shard_map.250.two = bf16[2,4,128,1024]{3,2,1,0:T(8,128)(2,1)} custom-call(bf16[2,4,128,640]{3,2,1,0:T(8,128)(2,1)} %get-tuple-element.44.both, bf16[640,1024]{1,0:T(8,128)(2,1)} %shard_map.248.tail), custom_call_target="tpu_custom_call" | custom-call | flops 2097152 | bytes 6144 | tf_op jit(solution)/shard_map/pallas_call | solution.py:294
  101.5 0.0 reduce-scatter.3.cloned.1.call-update
  101.5 0.0 all-gather.5.cloned.1.call-done.cot
  101.5 4.6 %shard_map.249 = (bf16[16,80,512]{2,1,0:T(8,128)(2,1)}, f32[8,1024]{1,0:T(8,128)}) custom-call(bf16[1024,640]{1,0:T(8,128)(2,1)} %bitcast.24, bf16[1024,1024]{1,0:T(8,128)(2,1)} %all-gather.5.cloned.1.call-done.cot), custom_call_target="tpu_custom_call" | custom-call | flops 2097152 | bytes 6144 | tf_op jit(solution)/shard_map/pallas_call | solution.py:429
  106.1 3.7 %all-to-all-start.2 = ((bf16[16,80,512]{2,1,0:T(8,128)(2,1)}), bf16[16,80,512]{2,1,0:T(8,128)(2,1)S(1)}, u32[]{:S(2)}, u32[]{:S(2)}) async-start(bf16[16,80,512]{2,1,0:T(8,128)(2,1)} %get-tuple-element.46.one), calls=%async_computation.3 | async-start | bytes 2621440 | tf_op jit(solution)/shard_map/all_to_all | solution.py:33
  109.8 0.0 reduce-scatter.5.cloned.1.call-start
  109.9 19.3 %shard_map.251 = (bf16[2,4,128,1024]{3,2,1,0:T(8,128)(2,1)}, bf16[1024,1024]{1,0:T(8,128)(2,1)}) custom-call(s32[6]{0:T(128)} %stack.27.at, bf16[2,4,128,384]{3,2,1,0:T(8,128)(2,1)} %get-tuple-element.38.rotated, f32[2,4,128,128]{3,2,1,0:T(8,128)} %get-tuple-element.39.sums, f32[2,4,128,512]{3,2,1,0:T(8,128)} %get-tuple-element.40.ahead.slope, ...), custom_call_target="tpu_custom_call" | custom-call | flops 6291456 | bytes 16384 | tf_op jit(solution)/shard_map/pallas_call | solution.py:387
  129.1 0.0 all-to-all-done.2
  129.1 0.0 reduce-scatter.3.cloned.1.call-done.mixed_sum
  129.2 0.0 reduce-scatter.5.cloned.1.call-update
  129.2 10.5 %all-to-all-start.3 = ((bf16[64,16,1024]{2,1,0:T(8,128)(2,1)}), bf16[64,16,1024]{2,1,0:T(8,128)(2,1)S(1)}, u32[]{:S(2)}, u32[]{:S(2)}) async-start(bf16[64,16,1024]{2,1,0:T(8,128)(2,1)} %bitcast.27), calls=%async_computation.5 | async-start | bytes 4194304 | tf_op jit(solution)/shard_map/all_to_all | solution.py:33
  139.7 0.2 reduce_sum.22
  139.9 3.5 %collective-permute-start.2 = (bf16[80,512]{1,0:T(8,128)(2,1)S(1)}, bf16[80,512]{1,0:T(8,128)(2,1)S(1)}, u32[]{:S(2)}, u32[]{:S(2)}) collective-permute-start(bf16[80,512]{1,0:T(8,128)(2,1)S(1)} %reduce_sum.22), channel_id=1, source_target_pairs={{0,0},{4,1},{8,2},{12,3},{16,4},{20,5},{24,6},{28,7},{1,8},{5,9},{... | collective-permute-start | bytes 245768 | tf_op jit(solution)/shard_map/ppermute | solution.py:544
  143.5 4.0 %collective-permute-start.3 = (bf16[80,512]{1,0:T(8,128)(2,1)S(1)}, bf16[80,512]{1,0:T(8,128)(2,1)S(1)}, u32[]{:S(2)}, u32[]{:S(2)}) collective-permute-start(bf16[80,512]{1,0:T(8,128)(2,1)S(1)} %reduce_sum.22), channel_id=1, source_target_pairs={{0,64},{4,65},{8,66},{12,67},{16,68},{20,69},{24,70},{28,71},{1,72... | collective-permute-start | bytes 245768 | tf_op jit(solution)/shard_map/ppermute | solution.py:545
  147.5 20.7 %collective-permute-done.2 = bf16[80,512]{1,0:T(8,128)(2,1)S(1)} collective-permute-done((bf16[80,512]{1,0:T(8,128)(2,1)S(1)}, bf16[80,512]{1,0:T(8,128)(2,1)S(1)}, u32[]{:S(2)}, u32[]{:S(2)}) %collective-permute-start.2) | collective-permute-done | bytes 81952 | tf_op jit(solution)/shard_map/ppermute | solution.py:544
  168.2 7.4 %collective-permute-done.3 = bf16[80,512]{1,0:T(8,128)(2,1)S(1)} collective-permute-done((bf16[80,512]{1,0:T(8,128)(2,1)S(1)}, bf16[80,512]{1,0:T(8,128)(2,1)S(1)}, u32[]{:S(2)}, u32[]{:S(2)}) %collective-permute-start.3) | collective-permute-done | bytes 81952 | tf_op jit(solution)/shard_map/ppermute | solution.py:545
  175.7 0.0 all-to-all-done.3
  175.7 0.4 convert_reduce_fusion
  176.1 0.0 copy-start.2
  176.1 1.7 collective-permute-start.1
  177.8 0.6 maximum_convert_fusion
  178.4 0.7 fusion.4
  179.1 3.9 %collective-permute-done.1.far = bf16[4,16,1024]{2,1,0:T(8,128)(2,1)S(1)} collective-permute-done((bf16[4,16,1024]{2,1,0:T(8,128)(2,1)S(1)}, bf16[4,16,1024]{2,1,0:T(8,128)(2,1)S(1)}, u32[]{:S(2)}, u32[]{:S(2)}) %collective-permute-start.1) | collective-permute-done | bytes 131104 | tf_op jit(solution)/shard_map/ppermute | solution.py:29
  183.1 0.0 copy-start.3
  183.1 0.0 copy-done.2
  183.1 0.7 copy-done.3
  183.7 1.8 shard_map.253
  185.5 0.0 copy-start.6
  185.6 6.8 %reduce-scatter.5.cloned.1.call-done.norm_grad = bf16[128,1024]{1,0:T(8,128)(2,1)} async-done(((bf16[1024,1024]{1,0:T(8,128)(2,1)}), bf16[128,1024]{1,0:T(8,128)(2,1)}) %reduce-scatter.5.cloned.1.call-update) | async-done | bytes 262160 | tf_op jit(solution)/shard_map/reduce_scatter | solution.py:470
  192.3 3.2 %shard_map.252 = (bf16[128,1024]{1,0:T(8,128)(2,1)}, f32[128,1024]{1,0:T(8,128)}) custom-call(s32[6]{0:T(128)} %stack.27.at, bf16[128,1024]{1,0:T(8,128)(2,1)} %tokens.3, bf16[128,1024]{1,0:T(8,128)(2,1)} %out_grad.1, bf16[128,1024]{1,0:T(8,128)(2,1)} %reduce-scatter.5.cloned.1.call-done.norm_grad, ...), custom_call_target="tpu_custom_call" | custom-call | bytes 1024 | tf_op jit(solution)/shard_map/pallas_call | solution.py:49
  195.5 0.0 copy-done.6
  195.5 0.5 copy.29
  (7 shorter events, 0.1 us)
Async XLA Ops:
  7.2 63.9 %all-gather.3.cloned.1.call-start = ((), (), s32[]{:S(2)}) async-start(), calls=%async_computation.6 | async-start | bytes 2359296 | tf_op jit(solution)/shard_map/all_gather | solution.py:466
  9.8 91.7 %all-gather.5.cloned.1.call-start = ((), (), s32[]{:S(2)}) async-start(), calls=%async_computation.7 | async-start | bytes 2359296 | tf_op jit(solution)/shard_map/all_gather | solution.py:466
  13.9 11.0 %copy-start.4 = (bf16[64,1024]{1,0:T(8,128)(2,1)S(1)}, bf16[64,1024]{1,0:T(8,128)(2,1)}, u32[]{:S(2)}) copy-start(bf16[64,1024]{1,0:T(8,128)(2,1)} %param.25) | copy-start | bytes 393220
  13.9 11.0 %copy-start.5 = (bf16[16,1024]{1,0:T(8,128)(2,1)S(1)}, bf16[16,1024]{1,0:T(8,128)(2,1)}, u32[]{:S(2)}) copy-start(bf16[16,1024]{1,0:T(8,128)(2,1)} %param.21) | copy-start | bytes 98308
  13.9 45.5 %all-to-all-start = ((bf16[64,16,1024]{2,1,0:T(8,128)(2,1)}), bf16[64,16,1024]{2,1,0:T(8,128)(2,1)S(1)}, u32[]{:S(2)}, u32[]{:S(2)}) async-start(bf16[64,16,1024]{2,1,0:T(8,128)(2,1)} %shard_map.246), calls=%async_computation | async-start | bytes 4194304 | tf_op jit(solution)/shard_map/all_to_all | solution.py:33
  25.0 23.7 %collective-permute-start = (bf16[80,512]{1,0:T(8,128)(2,1)S(1)}, bf16[80,512]{1,0:T(8,128)(2,1)S(1)}, u32[]{:S(2)}, u32[]{:S(2)}) collective-permute-start(bf16[80,512]{1,0:T(8,128)(2,1)S(1)} %fusion.5), channel_id=1, source_target_pairs={{0,0},{1,4},{2,8},{3,12},{4,16},{5,20},{6,24},{7,28},{8,1},{9,5},{... | collective-permute-start | bytes 245768 | tf_op jit(solution)/shard_map/ppermute | solution.py:512
  59.5 11.6 %copy-start = (bf16[64,16,1024]{2,1,0:T(8,128)(2,1)}, bf16[64,16,1024]{2,1,0:T(8,128)(2,1)S(1)}, u32[]{:S(2)}) copy-start(bf16[64,16,1024]{2,1,0:T(8,128)(2,1)S(1)} %all-to-all-done) | copy-start | bytes 6291460
  60.8 31.8 %all-to-all-start.1 = ((bf16[16,80,512]{2,1,0:T(8,128)(2,1)}), bf16[16,80,512]{2,1,0:T(8,128)(2,1)S(1)}, u32[]{:S(2)}, u32[]{:S(2)}) async-start(bf16[16,80,512]{2,1,0:T(8,128)(2,1)} %broadcast_in_dim.43), calls=%async_computation.1 | async-start | bytes 2621440 | tf_op jit(solution)/shard_map/all_to_all | solution.py:33
  69.7 59.4 %reduce-scatter.3.cloned.1.call-start = ((), (), s32[]{:S(2)}) async-start(), calls=%async_computation.8 | async-start | bytes 2359296 | tf_op jit(solution)/shard_map/reduce_scatter | solution.py:470
  92.7 1.1 copy-start.1
  106.1 23.0 %all-to-all-start.2 = ((bf16[16,80,512]{2,1,0:T(8,128)(2,1)}), bf16[16,80,512]{2,1,0:T(8,128)(2,1)S(1)}, u32[]{:S(2)}, u32[]{:S(2)}) async-start(bf16[16,80,512]{2,1,0:T(8,128)(2,1)} %get-tuple-element.46.one), calls=%async_computation.3 | async-start | bytes 2621440 | tf_op jit(solution)/shard_map/all_to_all | solution.py:33
  109.8 82.5 %reduce-scatter.5.cloned.1.call-start = ((), (), s32[]{:S(2)}) async-start(), calls=%async_computation.9 | async-start | bytes 2359296 | tf_op jit(solution)/shard_map/reduce_scatter | solution.py:470
  129.2 46.5 %all-to-all-start.3 = ((bf16[64,16,1024]{2,1,0:T(8,128)(2,1)}), bf16[64,16,1024]{2,1,0:T(8,128)(2,1)S(1)}, u32[]{:S(2)}, u32[]{:S(2)}) async-start(bf16[64,16,1024]{2,1,0:T(8,128)(2,1)} %bitcast.27), calls=%async_computation.5 | async-start | bytes 4194304 | tf_op jit(solution)/shard_map/all_to_all | solution.py:33
  139.9 28.3 %collective-permute-start.2 = (bf16[80,512]{1,0:T(8,128)(2,1)S(1)}, bf16[80,512]{1,0:T(8,128)(2,1)S(1)}, u32[]{:S(2)}, u32[]{:S(2)}) collective-permute-start(bf16[80,512]{1,0:T(8,128)(2,1)S(1)} %reduce_sum.22), channel_id=1, source_target_pairs={{0,0},{4,1},{8,2},{12,3},{16,4},{20,5},{24,6},{28,7},{1,8},{5,9},{... | collective-permute-start | bytes 245768 | tf_op jit(solution)/shard_map/ppermute | solution.py:544
  143.5 32.2 %collective-permute-start.3 = (bf16[80,512]{1,0:T(8,128)(2,1)S(1)}, bf16[80,512]{1,0:T(8,128)(2,1)S(1)}, u32[]{:S(2)}, u32[]{:S(2)}) collective-permute-start(bf16[80,512]{1,0:T(8,128)(2,1)S(1)} %reduce_sum.22), channel_id=1, source_target_pairs={{0,64},{4,65},{8,66},{12,67},{16,68},{20,69},{24,70},{28,71},{1,72... | collective-permute-start | bytes 245768 | tf_op jit(solution)/shard_map/ppermute | solution.py:545
  176.1 7.0 %copy-start.2 = (f32[2,2,16,1024]{3,2,1,0:T(8,128)}, f32[2,2,16,1024]{3,2,1,0:T(8,128)S(1)}, u32[]{:S(2)}) copy-start(f32[2,2,16,1024]{3,2,1,0:T(8,128)S(1)} %convert_reduce_fusion) | copy-start | bytes 786436
  176.1 7.0 %collective-permute-start.1 = (bf16[4,16,1024]{2,1,0:T(8,128)(2,1)S(1)}, bf16[4,16,1024]{2,1,0:T(8,128)(2,1)S(1)}, u32[]{:S(2)}, u32[]{:S(2)}) collective-permute-start(bf16[4,16,1024]{2,1,0:T(8,128)(2,1)S(1)} %bitcast_convert_fusion), channel_id=1, source_target_pairs={{0,64},{64,0},{1,65},{65,1},{2,66},{66,2},{3,67},{67,3},{4,68},{68... | collective-permute-start | bytes 393224 | tf_op jit(solution)/shard_map/ppermute | solution.py:29
  183.1 0.7 copy-start.3
  185.5 10.0 %copy-start.6 = (f32[16]{0:T(128)S(1)}, f32[16]{0:T(128)}, u32[]{:S(2)}) copy-start(f32[16]{0:T(128)} %get-tuple-element.96) | copy-start | bytes 196
Sparse Core Ops, SparseCore 0:
  10.3 49.0 all-gather.2
  61.2 27.3 all-gather.4
  101.6 27.0 reduce-scatter.2
  130.9 61.3 reduce-scatter.4
where the time goes:
time: 203 us
  waiting for transfers between devices  79.9 us (39%)
  Pallas kernels  52.6 us (26%)
  starting transfers between devices  48.6 us (24%)
  between operations  14 us (7%)
  local copies, waits for them, and re-layouts  4.23 us (2%)
  other arithmetic  3.27 us (2%)
    all_to_all x4, starting transfers between devices, spread(): return lax.all_to_all(blocks, axes, split_axis=0, concat_axis=0, tiled=True)  34.1 us
    all_to_all x4, waiting for transfers between devices, spread(): return lax.all_to_all(blocks, axes, split_axis=0, concat_axis=0, tiled=True)  21.7 us
    ppermute x1, waiting for transfers between devices, local(): mine = lax.ppermute(tail_sum, AXES, [(b, a) for a, b in straight])  20.7 us
    pallas_call x1, Pallas kernels, backward(): pl.pallas_call(backward_body, grid=(8,), out_shape=(token_shape(WIDTH, BF...  19.3 us
    ppermute x1, waiting for transfers between devices, local(): tail = lax.ppermute(tail, AXES, straight)  18.6 us
    pallas_call x1, Pallas kernels, forward(): pl.pallas_call(forward_body, grid=(4,), out_shape=(token_shape(QKV, BF16)...  10.7 us
    ppermute x1, waiting for transfers between devices, local(): other = lax.ppermute(tail_sum, AXES, [(b, a) for a, b in crossed])  7.43 us
    pallas_call x3, Pallas kernels, call(): pl.pallas_call(body, out_shape=out_shape, in_specs=[smem()] + [vmem()] *...  6.96 us
  transfers between devices with their start and end apart: 12, of which 7 were waited for; matrix products, arithmetic and copies ran while one was open for 2% of the time, Pallas kernels for 23%

commit v1 on v0

v1 whole, which is shorter than its diff:
```python
import jax
import jax.numpy as jnp
from jax import lax
from jax.experimental import pallas as pl
from jax.experimental.pallas import tpu as pltpu
from jax.sharding import Mesh
from jax.sharding import PartitionSpec as P

HEADS = 16
HEAD_DIM = 64
ROT = 16
WIDTH = 1024
FF = 4096
TOK = 128
F32 = jnp.float32
BF16 = jnp.bfloat16
EPSILON = 1e-05
AXES = ("s", "yl", "z", "x", "c")
GROUP = ("s", "yl", "c")
PAIR = ("yl", "c")
PLACES = ("z", "x")
QKV = 384
HID = 512
COLS = QKV + HID
COUNTS = (1, 1, 1, 1, 1, 1, 3, 4)
VMEM_LIMIT = 60 * 1024 * 1024


def exchange(values, axes, count, mask):
    return lax.ppermute(values, axes, [(i, i ^ mask) for i in range(count)])


def spread(blocks, axes):
    return lax.all_to_all(blocks, axes, split_axis=0, concat_axis=0, tiled=True)


def after(values, first):
    return lax.optimization_barrier((values, first))[0]


def smem():
    return pl.BlockSpec(memory_space=pltpu.SMEM)


def vmem():
    return pl.BlockSpec(memory_space=pltpu.VMEM)


def call(body, out_shape, operands, ordered=False):
    return pl.pallas_call(
        body,
        out_shape=out_shape,
        in_specs=[smem()] + [vmem()] * (len(operands) - 1 - ordered) + [pl.BlockSpec(memory_space=pl.ANY)] * ordered,
        out_specs=jax.tree.map(lambda _: vmem(), out_shape),
        compiler_params=pltpu.CompilerParams(vmem_limit_bytes=VMEM_LIMIT),
        cost_estimate=pl.CostEstimate(flops=0, bytes_accessed=1 << 10, transcendentals=0),
    )(*operands)


def columns_of(vector, count):
    size = 16 * count
    wide = jnp.broadcast_to(vector[...].astype(F32)[None, :], (16, size))
    row = lax.broadcasted_iota(jnp.int32, (16, size), 0)
    lane = lax.broadcasted_iota(jnp.int32, (16, size), 1)
    return [
        jnp.sum(jnp.where(lane == row * count + i, wide, 0.0), axis=1, keepdims=True) for i in range(count)
    ]


def pack_body(at, *refs):
    vectors, out, copies, done = refs[:10], refs[10], refs[11:21], refs[21]
    qkv, fc_in = copies[8:]
    started = [pltpu.make_async_copy(a, b, done.at[i]) for i, (a, b) in enumerate(zip(vectors, copies))]
    for copy in started:
        copy.start()
    for copy in started:
        copy.wait()
    lane = lax.broadcasted_iota(jnp.int32, (16, 128), 1)
    small = jnp.zeros((16, 128), F32)
    columns = []
    for vector, count in zip(copies, COUNTS):
        columns += columns_of(vector, count)
    for index, column in enumerate(columns):
        small = jnp.where(lane == index, column, small)
    small = small.astype(BF16)
    for d in range(4):
        rank = lax.bitwise_xor(at[5], d)
        parts = []
        for part in range(3):
            first = pl.multiple_of(part * WIDTH + rank * 128, 128)
            parts.append(qkv[:, pl.ds(first, 128)])
        parts += [small, fc_in[:, pl.ds(pl.multiple_of(rank * HID, HID), HID)]]
        out[d] = jnp.concatenate(parts, axis=1)


def pack(at, qkv_weight, fc_in_weight, vectors):
    anywhere = pl.BlockSpec(memory_space=pltpu.HBM)
    return pl.pallas_call(
        pack_body,
        out_shape=jax.ShapeDtypeStruct((4, 16, WIDTH), BF16),
        in_specs=[smem()] + [anywhere] * 10,
        out_specs=vmem(),
        scratch_shapes=[pltpu.VMEM((16 * count,), BF16) for count in COUNTS]
        + [pltpu.VMEM((16, 3 * WIDTH), BF16), pltpu.VMEM((16, FF), BF16), pltpu.SemaphoreType.DMA((10,))],
        compiler_params=pltpu.CompilerParams(vmem_limit_bytes=VMEM_LIMIT),
        cost_estimate=cost(0, 0),
    )(at, *vectors, qkv_weight, fc_in_weight)


def norm_stats(tokens):
    inputs = tokens[...].astype(F32)
    centered = inputs - jnp.mean(inputs, axis=1, keepdims=True)
    inverse = lax.rsqrt(jnp.mean(centered * centered, axis=1, keepdims=True) + EPSILON)
    return inputs, centered * inverse, inverse


def norm_body(at, tokens, ahead, out):
    out[...] = norm_stats(tokens)[1].astype(BF16)


def outputs_body(at, tokens, out_grad, norm_grad, mixed_sum, columns, mixed, tokens_grad):
    inputs, normed, inverse = norm_stats(tokens)
    sel = lax.broadcasted_iota(jnp.int32, (8, 128), 1)
    sel = jnp.where((sel == 4) | (sel == 5), 1.0, 0.0).astype(BF16)
    bias = nt_dot(sel, columns[:, QKV:512])[0:1]
    mixed[...] = (inputs + mixed_sum[...].astype(F32) + bias).astype(BF16)
    grad = norm_grad[...].astype(F32)
    mean_grad = jnp.mean(grad, axis=1, keepdims=True)
    mean_dot = jnp.mean(grad * normed, axis=1, keepdims=True)
    tokens_grad[...] = out_grad[...].astype(F32) + inverse * (grad - mean_grad - normed * mean_dot)


def owner_body(at, *refs):
    pieces, mine, other, ahead = refs[:4]
    (qkv_out, in_out, g1, b1, g2, b2, bias, same, qb, fb, dense_out, fc_out) = refs[4:]
    for half, part in ((at[0], mine), (1 - at[0], other)):
        lanes = pl.ds(pl.multiple_of(half * 512, 512), 512)
        dense_out[:, lanes] = part[0:16].astype(F32)
        fc_out[:, lanes] = part[16:80].astype(F32)
    small = jnp.zeros((16, 128), F32)
    for rank in range(8):
        block = pieces[rank]
        for part in range(3):
            first = part * WIDTH + rank * 128
            qkv_out[:, first : first + 128] = block[:, part * 128 : part * 128 + 128].astype(F32)
        small = small + block[:, QKV:512].astype(F32)
        in_out[:, rank * HID : rank * HID + HID] = block[:, 512:].astype(F32)
    lane = 0
    for vector, count in ((g1, 1), (b1, 1), (g2, 1), (b2, 1), (bias, 1), (None, 1), (qb, 3), (fb, 4)):
        if vector is not None:
            size = 16 * count
            row = lax.broadcasted_iota(jnp.int32, (16, size), 0)
            place = lax.broadcasted_iota(jnp.int32, (16, size), 1)
            total = jnp.zeros((16, size), F32)
            for i in range(count):
                total = jnp.where(place == row * count + i, small[:, lane + i : lane + i + 1], total)
            vector[...] = jnp.sum(total, axis=0)
            if vector is bias:
                same[...] = jnp.sum(total, axis=0)
        lane += count


def nt_dot(left, right):
    return lax.dot_general(left, right, (((1,), (1,)), ((), ())), preferred_element_type=F32)


def tn_dot(left, right):
    return lax.dot_general(left, right, (((0,), (0,)), ((), ())), preferred_element_type=F32)


def dot(left, right):
    return jnp.dot(left, right, preferred_element_type=F32)


def bias_places(rank, shape, dim):
    column = lax.broadcasted_iota(jnp.int32, shape, dim)
    part, within = lax.shift_right_logical(column, 7), lax.bitwise_and(column, 127)
    q_column = part * WIDTH + rank * 128 + within
    h_column = rank * HID + column - QKV
    q_row = lax.div(q_column, 3)
    is_q = column < QKV
    row = jnp.where(is_q, q_row, lax.shift_right_logical(h_column, 2))
    lane = jnp.where(is_q, 6 + q_column - 3 * q_row, 9 + lax.bitwise_and(h_column, 3))
    return row, lane


def turn(values, cosine, low, high, sign):
    back = pltpu.roll(values, 128 - 8, 1)
    ahead = pltpu.roll(values, 8, 1)
    return values * cosine + sign * (back * low + ahead * high)


def causal():
    row = lax.broadcasted_iota(jnp.int32, (256, 256), 0)
    return row >= lax.broadcasted_iota(jnp.int32, (256, 256), 1)


def owner_rows(at, place, d):
    pair = lax.bitwise_xor(at[1] * 2 + at[4], d)
    return pl.multiple_of((lax.shift_right_logical(pair, 1) * 16 + place) * 32 + lax.bitwise_and(pair, 1) * 16, 16)


def forward_body(at, xh, pieces, cos, sin_low, sin_high, rotated, sums, both, slope, turned, columns, hot, flipped, scaled, bias):
    rank = at[5]

    @pl.when(pl.program_id(0) == 0)
    def _():
        for place in range(16):
            for d in range(4):
                columns[pl.ds(owner_rows(at, place, d), 16), :] = pieces[place, d]
        params = columns[:, QKV:512]
        weights = jnp.concatenate([columns[:, :QKV], columns[:, 512:]], axis=1)
        row, lane = bias_places(rank, (WIDTH, COLS), 1)
        hot[...] = (lax.broadcasted_iota(jnp.int32, (WIDTH, COLS), 0) == row).astype(F32).astype(BF16)
        row, lane = bias_places(rank, (128, COLS), 1)
        sub = lax.broadcasted_iota(jnp.int32, (128, COLS), 0)
        column = lax.broadcasted_iota(jnp.int32, (128, COLS), 1)
        own = jnp.where(sub == lane, tn_dot(params, hot[...]), 0.0)
        shifted = jnp.where(sub == jnp.where(column < QKV, 1, 3), tn_dot(params, weights), 0.0)
        bias[...] = jnp.sum(own + shifted, axis=0, keepdims=True)
        gains = params.astype(F32)
        scaled[:, :QKV] = (weights[:, :QKV].astype(F32) * gains[:, 0:1]).astype(BF16)
        scaled[:, QKV:] = (weights[:, QKV:].astype(F32) * gains[:, 2:3]).astype(BF16)
        turned[...] = scaled[...].T

    tokens = xh[...].reshape(256, WIDTH)
    for piece in range(2):
        first = pl.multiple_of(piece * 512 + pl.program_id(0) * TOK, TOK)
        flipped[:, pl.ds(first, TOK)] = tokens[piece * TOK : piece * TOK + TOK].T
    proj = dot(tokens, scaled[:, :QKV]) + bias[:, :QKV]
    table = cos[...], sin_low[...], sin_high[...]
    queries = turn(proj[:, 0:128], *table, 1.0).astype(BF16)
    keys = turn(proj[:, 128:256], *table, 1.0).astype(BF16)
    values = proj[:, 256:384].astype(BF16)
    rotated[...] = jnp.concatenate([queries, keys, values], axis=1).reshape(rotated.shape)
    allowed = causal()
    outs, logs = [], []
    for h in range(2):
        lanes = slice(h * HEAD_DIM, (h + 1) * HEAD_DIM)
        scores = jnp.where(allowed, nt_dot(queries[:, lanes], keys[:, lanes]) * HEAD_DIM ** (-0.5), -1e30)
        peak = jnp.max(scores, axis=1, keepdims=True)
        weights = jnp.exp(scores - peak)
        norm = jnp.sum(weights, axis=1, keepdims=True)
        outs.append(dot((weights / norm).astype(BF16), values[:, lanes]))
        logs.append(jnp.broadcast_to(peak + jnp.log(norm), (256, HEAD_DIM)))
    sums[...] = jnp.concatenate(logs, axis=1).reshape(sums.shape)
    attended = jnp.concatenate(outs, axis=1).astype(BF16)
    hidden = dot(tokens, scaled[:, QKV:]) + bias[:, QKV:]
    cdf = 0.5 * (1.0 + lax.erf(hidden * (0.5**0.5)))
    both[...] = jnp.concatenate([attended, (hidden * cdf).astype(BF16)], axis=1).reshape(both.shape)
    slope[...] = (cdf + hidden * jnp.exp(-0.5 * hidden * hidden) * 0.3989422804014327).astype(BF16).reshape(slope.shape)


def token_spec(lanes):
    return pl.BlockSpec((2, 1, TOK, lanes), lambda i: (0, i, 0, 0))


def token_shape(lanes, dtype):
    return jax.ShapeDtypeStruct((2, 4, TOK, lanes), dtype)


def whole(rows, lanes):
    return pl.BlockSpec((rows, lanes), lambda i: (0, 0))


def cost(flops, size):
    return pl.CostEstimate(flops=flops >> 10, bytes_accessed=size >> 10, transcendentals=0)


def forward(at, xh, pieces, tables):
    table = whole(256, 128)
    return pl.pallas_call(
        forward_body,
        grid=(4,),
        out_shape=(
            token_shape(QKV, BF16),
            token_shape(128, F32),
            token_shape(128 + HID, BF16),
            token_shape(HID, BF16),
            jax.ShapeDtypeStruct((COLS, WIDTH), BF16),
            jax.ShapeDtypeStruct((WIDTH, WIDTH), BF16),
            jax.ShapeDtypeStruct((WIDTH, COLS), BF16),
            jax.ShapeDtypeStruct((WIDTH, WIDTH), BF16),
        ),
        in_specs=[
            smem(),
            token_spec(WIDTH),
            pl.BlockSpec((16, 4, 16, WIDTH), lambda i: (0, 0, 0, 0)),
            table,
            table,
            table,
        ],
        out_specs=(
            token_spec(QKV),
            token_spec(128),
            token_spec(128 + HID),
            token_spec(HID),
            whole(COLS, WIDTH),
            whole(WIDTH, WIDTH),
            whole(WIDTH, COLS),
            whole(WIDTH, WIDTH),
        ),
        scratch_shapes=[pltpu.VMEM((WIDTH, COLS), BF16), pltpu.VMEM((1, COLS), F32)],
        compiler_params=pltpu.CompilerParams(vmem_limit_bytes=VMEM_LIMIT),
        cost_estimate=cost(4 << 30, 8 << 20),
    )(at, xh, pieces, *tables)


def mixed_body(both, blocks, ahead, out_ref, turned, both_here, blocks_here, tail, buffer, done, written):
    started = fetch((blocks, both), (blocks_here, both_here), done)
    started[0].wait()
    for place in range(16):
        k, lane = place // 2, (place % 2) * 512
        tail[k * 16 : k * 16 + 16, lane : lane + 512] = blocks_here[place, 0:16, :]
        tail[128 + k * 64 : 192 + k * 64, lane : lane + 512] = blocks_here[place, 16:80, :]
    started[1].wait()
    stores = []
    for i in range(4):
        product = dot(both_here[:, i].reshape(256, 128 + HID), tail[...])
        buffer[:, i] = product.astype(BF16).reshape(2, TOK, WIDTH)
        stores.append(pltpu.make_async_copy(buffer.at[:, i], out_ref.at[:, i], written.at[i]))
        stores[-1].start()
    turned[...] = tail[...].T
    for copy in stores:
        copy.wait()


def mixed_of(both, blocks, ahead):
    remote = pl.BlockSpec(memory_space=pltpu.HBM)
    return pl.pallas_call(
        mixed_body,
        out_shape=(token_shape(WIDTH, BF16), jax.ShapeDtypeStruct((WIDTH, 640), BF16)),
        in_specs=[remote, remote, pl.BlockSpec(memory_space=pl.ANY)],
        out_specs=(remote, vmem()),
        scratch_shapes=[
            pltpu.VMEM(both.shape, BF16),
            pltpu.VMEM(blocks.shape, BF16),
            pltpu.VMEM((640, WIDTH), BF16),
            pltpu.VMEM((2, 4, TOK, WIDTH), BF16),
            pltpu.SemaphoreType.DMA((2,)),
            pltpu.SemaphoreType.DMA((4,)),
        ],
        compiler_params=pltpu.CompilerParams(vmem_limit_bytes=VMEM_LIMIT),
        cost_estimate=cost(2 << 30, 6 << 20),
    )(both, blocks, ahead)


def sequence_step(packed, logs, slope, cotangent, tail, table):
    grad = dot(cotangent, tail[:, :128]).astype(BF16)
    dhid = (dot(cotangent, tail[:, 128:]) * slope.astype(F32)).astype(BF16)
    allowed = causal()
    dqs, dks, dvs = [], [], []
    scale = HEAD_DIM ** (-0.5)
    for h in range(2):
        q, k, v = (packed[:, i * 128 + h * HEAD_DIM : i * 128 + (h + 1) * HEAD_DIM] for i in range(3))
        g = grad[:, h * HEAD_DIM : (h + 1) * HEAD_DIM]
        scores = nt_dot(q, k) * scale - logs[:, h * HEAD_DIM : h * HEAD_DIM + 1]
        probs = jnp.exp(jnp.where(allowed, scores, -1e30))
        dprobs = nt_dot(g, v)
        inner = jnp.sum(probs * dprobs, axis=1, keepdims=True)
        ds = (probs * (dprobs - inner)).astype(BF16)
        dqs.append(dot(ds, k) * scale)
        dks.append(tn_dot(ds, q) * scale)
        dvs.append(tn_dot(probs.astype(BF16), g))
    dq = turn(jnp.concatenate(dqs, axis=1).astype(BF16).astype(F32), *table, -1.0)
    dk = turn(jnp.concatenate(dks, axis=1).astype(BF16).astype(F32), *table, -1.0)
    dv = jnp.concatenate(dvs, axis=1)
    back = jnp.concatenate([dq.astype(BF16), dk.astype(BF16), dv.astype(BF16), dhid], axis=1)
    return back


def columns_step(rank, block, xh, columns, hot, total, grads, total_cols, spots):
    product = dot(xh, grads)
    params = columns[:, QKV:512].astype(F32)
    weights = jnp.concatenate([columns[:, :QKV], columns[:, 512:]], axis=1).astype(F32)
    small = nt_dot(hot, spots)
    lane = lax.broadcasted_iota(jnp.int32, (256, 128), 1)
    mirror = lax.broadcasted_iota(jnp.int32, (256, 256), 0) == lax.broadcasted_iota(jnp.int32, (256, 256), 1)
    mine = jnp.sum(jnp.where(mirror, total, 0.0), axis=1, keepdims=True)
    small = jnp.where((lane == 4) & (rank == 0), mine, small)
    changes = []
    for first, last, index in ((0, QKV, 0), (QKV, COLS, 2)):
        w, g, t = weights[:, first:last], product[:, first:last], total_cols[:, first:last]
        small = jnp.where(lane == index, jnp.sum(w * g, axis=1, keepdims=True), small)
        small = jnp.where(lane == index + 1, jnp.sum(w * t, axis=1, keepdims=True), small)
        change = (params[:, index : index + 1] * g + params[:, index + 1 : index + 2] * t).astype(BF16)
        changes.append(change)
    return jnp.concatenate([changes[0], small.astype(BF16), changes[1]], axis=1)


def fetch(sources, copies, done):
    started = [pltpu.make_async_copy(a, b, done.at[i]) for i, (a, b) in enumerate(zip(sources, copies))]
    for copy in started:
        copy.start()
    return started


def backward_body(at, *refs):
    sources, (norm_out, columns_out), copies = refs[:13], refs[15:17], refs[17:30]
    grads, norm_buffer, columns_buffer, done, written = refs[30:]
    cot, tail, rotated, sums, slope, cos, sin_low, sin_high, scaled, total, xh, columns, hot = copies
    started = fetch(sources, copies, done)
    for copy in started[:8]:
        copy.wait()
    table = cos[...], sin_low[...], sin_high[...]
    stores = []
    for i in range(4):
        back = sequence_step(
            rotated[:, i].reshape(256, QKV),
            sums[:, i].reshape(256, 128),
            slope[:, i].reshape(256, HID),
            cot[:, i].reshape(256, WIDTH),
            tail,
            table,
        )
        grads[:, i] = back.reshape(2, TOK, COLS)
        if i == 0:
            started[8].wait()
        norm_buffer[:, i] = dot(back, scaled[...]).astype(BF16).reshape(2, TOK, WIDTH)
        stores.append(pltpu.make_async_copy(norm_buffer.at[:, i], norm_out.at[:, i], written.at[i]))
        stores[-1].start()
    for copy in started[9:]:
        copy.wait()
    rank = at[5]
    every = grads[...].reshape(WIDTH, COLS)
    total_cols = dot(jnp.ones((8, WIDTH), BF16), every)[0:1]
    row, lane = bias_places(rank, (128, COLS), 1)
    sub = lax.broadcasted_iota(jnp.int32, (128, COLS), 0)
    spots = jnp.where(sub == lane, total_cols, 0.0).astype(BF16)
    for block in range(4):
        rows = slice(block * 256, block * 256 + 256)
        result = columns_step(
            rank, block, xh[rows], columns[rows], hot[rows], total[0:1, rows], every, total_cols, spots
        )
        place, pair = (block % 2) * 8, (block // 2) * 2
        for inside in range(16):
            columns_buffer[place + inside // 2, pair + inside % 2] = result[inside * 16 : inside * 16 + 16]
        here = (slice(place, place + 8), slice(pair, pair + 2))
        stores.append(pltpu.make_async_copy(columns_buffer.at[here], columns_out.at[here], written.at[4 + block]))
        stores[-1].start()
    for copy in stores:
        copy.wait()


def backward(at, *operands):
    remote = pl.BlockSpec(memory_space=pltpu.HBM)
    return pl.pallas_call(
        backward_body,
        out_shape=(token_shape(WIDTH, BF16), jax.ShapeDtypeStruct((16, 4, 16, WIDTH), BF16)),
        in_specs=[smem()] + [remote] * 13 + [pl.BlockSpec(memory_space=pl.ANY)] * 2,
        out_specs=(remote, remote),
        scratch_shapes=[pltpu.VMEM(a.shape, a.dtype) for a in operands[:13]]
        + [
            pltpu.VMEM((2, 4, TOK, COLS), BF16),
            pltpu.VMEM((2, 4, TOK, WIDTH), BF16),
            pltpu.VMEM((16, 4, 16, WIDTH), BF16),
            pltpu.SemaphoreType.DMA((13,)),
            pltpu.SemaphoreType.DMA((8,)),
        ],
        compiler_params=pltpu.CompilerParams(vmem_limit_bytes=VMEM_LIMIT),
        cost_estimate=cost(6 << 30, 16 << 20),
    )(at, *operands)


def tail_grad_body(both, cot, out, total):
    for half in range(2):
        product = tn_dot(both[...], cot[:, half * 512 : half * 512 + 512]).astype(BF16)
        for k in range(8):
            out[2 * k + half, 0:16, :] = product[k * 16 : k * 16 + 16]
            out[2 * k + half, 16:80, :] = product[128 + k * 64 : 192 + k * 64]
    total[...] = dot(jnp.ones((8, WIDTH), BF16), cot[...])


def tail_grad_of(both, cot):
    return pl.pallas_call(
        tail_grad_body,
        out_shape=(jax.ShapeDtypeStruct((16, 80, 512), BF16), jax.ShapeDtypeStruct((8, WIDTH), F32)),
        in_specs=[vmem(), vmem()],
        out_specs=(vmem(), vmem()),
        compiler_params=pltpu.CompilerParams(vmem_limit_bytes=VMEM_LIMIT),
        cost_estimate=cost(2 << 30, 6 << 20),
    )(both, cot)


def rotary_tables():
    position = jnp.arange(256).astype(F32)[:, None]
    lane = jnp.arange(128) % HEAD_DIM
    halves = (lane % (ROT // 2)).astype(F32)
    frequency = jnp.power(10000.0, -2.0 * halves / ROT)[None, :]
    angle = position * frequency
    cosine, sine = jnp.cos(angle), jnp.sin(angle)
    lane = lane[None, :]
    return (
        jnp.where(lane < ROT, cosine, 1.0),
        jnp.where(lane < ROT // 2, -sine, 0.0),
        jnp.where((lane >= ROT // 2) & (lane < ROT), sine, 0.0),
    )


def gather_tokens(block):
    return lax.all_gather(block, GROUP, axis=0, tiled=True)


def scatter_tokens(partial):
    return lax.psum_scatter(partial, GROUP, scatter_dimension=0, tiled=True)


def tail_routes():
    straight, crossed = [], []
    for s in range(2):
        for dp in range(64):
            rank, place = dp // 8, 2 * (dp % 8) + s
            target_dp = (((rank >> 1) & 1) * 16 + place) * 2 + (rank & 1)
            target = (rank >> 2) * 64 + target_dp
            straight.append((s * 64 + dp, target))
            crossed.append(((1 - s) * 64 + dp, target))
    return straight, crossed


def local(
    tokens,
    ln1_gain,
    ln1_bias,
    ln2_gain,
    ln2_bias,
    qkv_weight,
    qkv_bias,
    dense_weight,
    dense_bias,
    fc_in_weight,
    fc_in_bias,
    fc_out_weight,
    fc_out_bias,
    out_grad,
):
    s, yl, z, x, c = (lax.axis_index(a) for a in AXES)
    rank = s * 4 + yl * 2 + c
    at = jnp.stack([s, yl, z, x, c, rank]).astype(jnp.int32)
    straight, crossed = tail_routes()
    shape = jax.ShapeDtypeStruct

    vectors = (ln1_gain, ln1_bias, ln2_gain, ln2_bias, dense_bias, fc_out_bias, qkv_bias, fc_in_bias)
    sent = pack(at, qkv_weight, fc_in_weight, vectors)
    pieces = jnp.stack([sent[0]] + [exchange(sent[d], PAIR, 4, d) for d in range(1, 4)])
    pieces = spread(jnp.broadcast_to(pieces, (16, 4, 16, WIDTH)), PLACES)
    tail = jnp.concatenate([dense_weight, fc_out_weight], axis=0)
    tail = lax.dynamic_slice_in_dim(tail, s * 512, 512, axis=1)
    tail = lax.ppermute(tail, AXES, straight)
    tail = spread(after(jnp.broadcast_to(tail, (16, 80, 512)), pieces), PLACES)

    own_xh = call(norm_body, shape((TOK, WIDTH), BF16), (at, tokens, sent), ordered=True)
    xh = gather_tokens(own_xh)
    cot = gather_tokens(after(out_grad, own_xh))

    xh_tokens, cot_tokens = xh.reshape(2, 4, TOK, WIDTH), cot.reshape(2, 4, TOK, WIDTH)
    tables = rotary_tables()
    rotated, sums, both, slope, turned, columns_in, hot, flipped = forward(at, xh_tokens, pieces, tables)
    tail_grad, total = tail_grad_of(both.reshape(WIDTH, 640), cot)
    mixed_part, tail = mixed_of(both, tail, tail_grad)
    tail_parts = spread(tail_grad, PLACES)
    mixed_sum = scatter_tokens(mixed_part.reshape(WIDTH, WIDTH))
    norm_part, columns_grad = backward(
        at, cot_tokens, tail, rotated, sums, slope, *tables, turned, total, flipped, columns_in, hot, tail_grad, mixed_part
    )
    norm_part, columns_grad = after((norm_part, columns_grad), tail_parts)
    norm_grad = scatter_tokens(norm_part.reshape(WIDTH, WIDTH))
    tail_sum = jnp.sum(tail_parts.astype(F32), axis=0).astype(BF16)
    column_sum = jnp.sum(spread(columns_grad, PLACES).astype(F32), axis=0).astype(BF16)
    column_sum = after(column_sum, mixed_sum)
    parts = spread(jnp.concatenate([column_sum, column_sum], axis=0), GROUP)
    vector = shape((16,), F32)
    mixed, tokens_grad = call(
        outputs_body,
        (shape((TOK, WIDTH), BF16), shape((TOK, WIDTH), F32)),
        (at, tokens, out_grad, norm_grad, mixed_sum, columns_in),
    )
    mine = lax.ppermute(tail_sum, AXES, [(b, a) for a, b in straight])
    other = lax.ppermute(tail_sum, AXES, [(b, a) for a, b in crossed])
    qkv_grad, fc_in_grad, *vectors_grad, dense_grad, fc_out_grad = call(
        owner_body,
        (shape((16, 3 * WIDTH), F32), shape((16, FF), F32))
        + (vector,) * 6
        + (shape((48,), F32), shape((64,), F32), shape((16, WIDTH), F32), shape((64, WIDTH), F32)),
        (at, parts, mine, other, mixed),
        ordered=True,
    )
    g1_grad, b1_grad, g2_grad, b2_grad, bias_grad, same_grad, qb_grad, fb_grad = vectors_grad
    return (
        mixed,
        tokens_grad,
        g1_grad,
        b1_grad,
        g2_grad,
        b2_grad,
        qkv_grad,
        qb_grad,
        dense_grad,
        bias_grad,
        fc_in_grad,
        fb_grad,
        fc_out_grad,
        same_grad,
    )


def solution(mesh):
    grid = Mesh(mesh.devices.reshape(2, 2, 4, 4, 2), AXES)
    rows = P(AXES, None)
    vector = P(AXES[1:])
    matrix = P(AXES[1:], None)
    in_specs = (
        rows,
        vector,
        vector,
        vector,
        vector,
        matrix,
        vector,
        matrix,
        vector,
        matrix,
        vector,
        matrix,
        vector,
        rows,
    )
    out_specs = (
        rows,
        rows,
        vector,
        vector,
        vector,
        vector,
        matrix,
        vector,
        matrix,
        vector,
        matrix,
        vector,
        matrix,
        vector,
    )
    return jax.shard_map(local, mesh=grid, in_specs=in_specs, out_specs=out_specs, check_vma=False)
```

time: 203 us -> 188 us (0.926)
  waiting for transfers between devices: 79.9 us -> 36.8 us
  blocking collectives: 0 us -> 32.5 us
  starting transfers between devices: 48.6 us -> 43.9 us
  Pallas kernels: 52.6 us -> 50.1 us
  local copies, waits for them, and re-layouts: 4.23 us -> 6.33 us
    all_to_all x0 -> x1, blocking collectives: none -> 32.5 us  [spread(): return lax.all_to_all(blocks, axes, split_axis=0, concat_axis=0, tiled=True)]
    ppermute x1, waiting for transfers between devices: 20.7 us -> 0.01 us  [local(): mine = lax.ppermute(tail_sum, AXES, [(b, a) for a, b in straight])]
    all_to_all x4, waiting for transfers between devices: 21.7 us -> 4.28 us  [spread(): return lax.all_to_all(blocks, axes, split_axis=0, concat_axis=0, tiled=True)]
    reduce_scatter x2, waiting for transfers between devices: 6.77 us -> 0.02 us  [scatter_tokens(): return lax.psum_scatter(partial, GROUP, scatter_dimension=0, tiled=True)]
    all_to_all x4, starting transfers between devices: 34.1 us -> 28.2 us  [spread(): return lax.all_to_all(blocks, axes, split_axis=0, concat_axis=0, tiled=True)]
    pallas_call x4 -> x3, Pallas kernels: 30.3 us -> 24.9 us  [the longest x1 16.9 us: backward(): pl.pallas_call(backward_body, out_shape=(token_shape(WIDTH, BF16), jax.Sh...]
    ppermute x1, waiting for transfers between devices: 18.6 us -> 21.6 us  [local(): tail = lax.ppermute(tail, AXES, straight)]
    pallas_call x1, Pallas kernels: 10.7 us -> 13.4 us  [forward(): pl.pallas_call(forward_body, grid=(4,), out_shape=(token_shape(QKV, BF16)...]
  transfers between devices with their start and end apart: 12 -> 14, of which waited for: 7 -> 6; matrix products, arithmetic and copies ran while one was open for 2% -> 3% of each run, Pallas kernels for 23% -> 20%
where the time goes in v1:
time: 188 us; the launch traced here: 186 us
  Pallas kernels  50.1 us (27%)
  starting transfers between devices  43.9 us (23%)
  waiting for transfers between devices  36.8 us (20%)
  blocking collectives  32.5 us (17%)
  between operations  14 us (7%)
  local copies, waits for them, and re-layouts  6.33 us (3%)
  other arithmetic  2.66 us (1%)
    all_to_all x1, blocking collectives, spread(): return lax.all_to_all(blocks, axes, split_axis=0, concat_axis=0, tiled=True)  32.5 us
    all_to_all x4, starting transfers between devices, spread(): return lax.all_to_all(blocks, axes, split_axis=0, concat_axis=0, tiled=True)  28.2 us
    ppermute x1, waiting for transfers between devices, local(): tail = lax.ppermute(tail, AXES, straight)  21.6 us
    pallas_call x1, Pallas kernels, backward(): pl.pallas_call(backward_body, out_shape=(token_shape(WIDTH, BF16), jax.Sh...  16.9 us
    pallas_call x1, Pallas kernels, forward(): pl.pallas_call(forward_body, grid=(4,), out_shape=(token_shape(QKV, BF16)...  13.4 us
    ppermute x1, waiting for transfers between devices, local(): other = lax.ppermute(tail_sum, AXES, [(b, a) for a, b in crossed])  7.45 us
    pallas_call x3, Pallas kernels, call(): pl.pallas_call(body, out_shape=out_shape, in_specs=[smem()] + [vmem()] *...  7.1 us
    ppermute x1, starting transfers between devices, local(): tail = lax.ppermute(tail, AXES, straight)  5.88 us
  transfers between devices with their start and end apart: 14, of which 6 were waited for; matrix products, arithmetic and copies ran while one was open for 3% of the time, Pallas kernels for 20%

profile of v1, /device:TPU:1, one launch (start us, length us, event | category | flops | bytes accessed | tf_op | source)
XLA Modules:
  0.0 186.3 jit_solution(12138119537094802186)
XLA Ops:
  7.2 0.0 all-gather.5.cloned.1.call-start
  7.2 0.7 stack.39.at
  7.9 2.6 %shard_map.245.ahead = bf16[4,16,1024]{2,1,0:T(8,128)(2,1)} custom-call(s32[6]{0:T(128)} %stack.39.at, bf16[16]{0:T(256)(128)(2,1)} %refs_0_.1, bf16[16]{0:T(256)(128)(2,1)} %refs_1_.1, bf16[16]{0:T(256)(128)(2,1)} %refs_2_.1, bf16[16]{0:T(256)(128)(2,1)} %refs_3_.1, bf16[16]{0:T(256)(128)(2,1)} %refs_4_.1, bf16[16]{0:T(256)(128)(2,1)} %refs_5_.1, ...), custom_call_target="tpu_custom_call" | custom-call | tf_op jit(solution)/shard_map/pallas_call | solution.py:98
  10.5 1.9 %shard_map.246 = bf16[128,1024]{1,0:T(8,128)(2,1)} custom-call(s32[6]{0:T(128)} %stack.39.at, bf16[128,1024]{1,0:T(8,128)(2,1)} %tokens.3, bf16[4,16,1024]{2,1,0:T(8,128)(2,1)} %shard_map.245.ahead), custom_call_target="tpu_custom_call" | custom-call | bytes 1024 | tf_op jit(solution)/shard_map/pallas_call | solution.py:50
  12.4 0.0 all-gather.5.cloned.1.call-update
  12.4 0.0 all-gather.3.cloned.1.call-start
  12.5 0.7 all-gather.3.cloned.1.call-update
  13.2 0.8 fusion.9
  14.0 2.2 %collective-permute-start.1 = (bf16[16,1024]{1,0:T(8,128)(2,1)S(1)}, bf16[16,1024]{1,0:T(8,128)(2,1)S(1)}, u32[]{:S(2)}, u32[]{:S(2)}) collective-permute-start(bf16[16,1024]{1,0:T(8,128)(2,1)S(1)} %get-tuple-element.82), channel_id=1, source_target_pairs={{0,32},{1,33},{32,0},{33,1},{2,34},{3,35},{34,2},{35,3},{4,36},{5,... | collective-permute-start | bytes 98312 | tf_op jit(solution)/shard_map/ppermute | solution.py:30
  16.2 0.9 collective-permute-start.2
  17.1 0.0 collective-permute-start
  17.2 0.3 collective-permute-done.1
  17.5 2.4 %collective-permute-done.2 = bf16[16,1024]{1,0:T(8,128)(2,1)S(1)} collective-permute-done((bf16[16,1024]{1,0:T(8,128)(2,1)S(1)}, bf16[16,1024]{1,0:T(8,128)(2,1)S(1)}, u32[]{:S(2)}, u32[]{:S(2)}) %collective-permute-start.2) | collective-permute-done | bytes 32800 | tf_op jit(solution)/shard_map/ppermute | solution.py:30
  19.9 0.0 collective-permute-done
  20.0 1.6 broadcast_in_dim.41
  21.6 0.0 copy-start.3
  21.6 0.0 copy-start.6
  21.6 7.7 %all-to-all-start = ((bf16[16,4,16,1024]{3,2,1,0:T(8,128)(2,1)}), bf16[16,4,16,1024]{3,2,1,0:T(8,128)(2,1)S(1)}, u32[]{:S(2)}, u32[]{:S(2)}) async-start(bf16[16,4,16,1024]{3,2,1,0:T(8,128)(2,1)} %broadcast_in_dim.41), calls=%async_computation | async-start | bytes 4194304 | tf_op jit(solution)/shard_map/all_to_all | solution.py:34
  29.3 0.0 copy-done.3
  29.3 0.0 copy-done.6
  29.4 5.9 %collective-permute-start.3 = (bf16[80,512]{1,0:T(8,128)(2,1)S(1)}, bf16[80,512]{1,0:T(8,128)(2,1)S(1)}, u32[]{:S(2)}, u32[]{:S(2)}) collective-permute-start(bf16[80,512]{1,0:T(8,128)(2,1)S(1)} %fusion.4), channel_id=1, source_target_pairs={{0,0},{1,4},{2,8},{3,12},{4,16},{5,20},{6,24},{7,28},{8,1},{9,5},{... | collective-permute-start | bytes 245768 | tf_op jit(solution)/shard_map/ppermute | solution.py:548
  35.2 21.6 %collective-permute-done.3 = bf16[80,512]{1,0:T(8,128)(2,1)S(1)} collective-permute-done((bf16[80,512]{1,0:T(8,128)(2,1)S(1)}, bf16[80,512]{1,0:T(8,128)(2,1)S(1)}, u32[]{:S(2)}, u32[]{:S(2)}) %collective-permute-start.3) | collective-permute-done | bytes 81952 | tf_op jit(solution)/shard_map/ppermute | solution.py:548
  56.8 3.0 %all-to-all-done.pieces = bf16[16,4,16,1024]{3,2,1,0:T(8,128)(2,1)S(1)} async-done(((bf16[16,4,16,1024]{3,2,1,0:T(8,128)(2,1)}), bf16[16,4,16,1024]{3,2,1,0:T(8,128)(2,1)S(1)}, u32[]{:S(2)}, u32[]{:S(2)}) %all-to-all-start) | async-done | bytes 2097184 | tf_op jit(solution)/shard_map/all_to_all | solution.py:34
  59.8 0.0 copy-start
  59.8 1.4 broadcast_in_dim.47
  61.2 7.6 %all-to-all-start.1 = ((bf16[16,80,512]{2,1,0:T(8,128)(2,1)}), bf16[16,80,512]{2,1,0:T(8,128)(2,1)S(1)}, u32[]{:S(2)}, u32[]{:S(2)}) async-start(bf16[16,80,512]{2,1,0:T(8,128)(2,1)} %broadcast_in_dim.47), calls=%async_computation.1 | async-start | bytes 2621440 | tf_op jit(solution)/shard_map/all_to_all | solution.py:34
  68.8 0.0 reduce-scatter.5.cloned.1.call-start
  68.9 1.3 fusion
  70.2 0.0 copy-done
  70.2 0.0 all-gather.5.cloned.1.call-done
  70.2 13.4 %shard_map.247 = (bf16[2,4,128,384]{3,2,1,0:T(8,128)(2,1)}, f32[2,4,128,128]{3,2,1,0:T(8,128)}, bf16[2,4,128,640]{3,2,1,0:T(8,128)(2,1)}, bf16[2,4,128,512]{3,2,...) custom-call(s32[6]{0:T(128)} %stack.39.at, ...), custom_call_target="tpu_custom_call" | custom-call | flops 4194304 | bytes 8192 | tf_op jit(solution)/shard_map/pallas_call | solution.py:272
  83.6 0.0 all-gather.3.cloned.1.call-done.cot
  83.7 4.6 %shard_map.248 = (bf16[16,80,512]{2,1,0:T(8,128)(2,1)}, f32[8,1024]{1,0:T(8,128)}) custom-call(bf16[1024,640]{1,0:T(8,128)(2,1)} %bitcast.22, bf16[1024,1024]{1,0:T(8,128)(2,1)} %all-gather.3.cloned.1.call-done.cot), custom_call_target="tpu_custom_call" | custom-call | flops 2097152 | bytes 6144 | tf_op jit(solution)/shard_map/pallas_call | solution.py:475
  88.3 0.0 all-to-all-done.1.blocks
  88.3 0.0 copy-start.1
  88.3 1.1 copy-done.1
  89.4 5.5 %shard_map.249 = (bf16[2,4,128,1024]{3,2,1,0:T(8,128)(2,1)}, bf16[1024,640]{1,0:T(8,128)(2,1)}) custom-call(bf16[2,4,128,640]{3,2,1,0:T(8,128)(2,1)} %get-tuple-element.48.both, bf16[16,80,512]{2,1,0:T(8,128)(2,1)} %copy-done.1, bf16[16,80,512]{2,1,0:T(8,128)(2,1)} %get-tuple-element.50.ahead.refs_13_), custom_call_target="tpu_custom_call" | custom-call | flops 2097152 | bytes 6144 | tf_op jit(solution)/shard_map/pallas_call | solution.py:330
  94.9 0.0 reduce-scatter.5.cloned.1.call-update
  94.9 6.7 %all-to-all-start.2 = ((bf16[16,80,512]{2,1,0:T(8,128)(2,1)}), bf16[16,80,512]{2,1,0:T(8,128)(2,1)S(1)}, u32[]{:S(2)}, u32[]{:S(2)}) async-start(bf16[16,80,512]{2,1,0:T(8,128)(2,1)} %get-tuple-element.50.ahead.refs_13_), calls=%async_computation.2 | async-start | bytes 2621440 | tf_op jit(solution)/shard_map/all_to_all | solution.py:34
  101.6 0.2 reduce-scatter.3.cloned.1.call-start
  101.8 16.9 %shard_map.250 = (bf16[2,4,128,1024]{3,2,1,0:T(8,128)(2,1)}, bf16[16,4,16,1024]{3,2,1,0:T(8,128)(2,1)}) custom-call(s32[6]{0:T(128)} %stack.39.at, bf16[2,4,128,1024]{3,2,1,0:T(8,128)(2,1)} %bitcast.21, bf16[1024,640]{1,0:T(8,128)(2,1)} %get-tuple-element.51.refs_1_, bf16[2,4,128,384]{3,2,1,0:T(8,128)(2,1)} %get-tuple-element.52.refs_2_, ...), custom_call_target="tpu_custom_call" | custom-call | flops 6291456 | bytes 16384 | tf_op jit(solution)/shard_map/pallas_call | solution.py:447
  118.7 1.2 all-to-all-done.2
  119.9 0.0 reduce-scatter.3.cloned.1.call-update
  120.0 32.5 %all_to_all.25 = bf16[16,4,16,1024]{3,2,1,0:T(8,128)(2,1)S(1)} all-to-all(bf16[16,4,16,1024]{3,2,1,0:T(8,128)(2,1)} %get-tuple-element.66), channel_id=1, replica_groups=mesh['s'=2,'yl'=2,'z'=4,'x'=4,'c'=2] {'z','x'}, dimensions={0} | all-to-all | bytes 4194304 | tf_op jit(solution)/shard_map/all_to_all | solution.py:34
  152.5 0.4 reduce_sum.24
  152.9 0.0 reduce-scatter.5.cloned.1.call-done.mixed_sum
  152.9 0.7 pad_maximum_fusion
  153.6 6.2 %all-to-all-start.4 = ((bf16[8,16,1024]{2,1,0:T(8,128)(2,1)}), bf16[8,16,1024]{2,1,0:T(8,128)(2,1)S(1)}, u32[]{:S(2)}, u32[]{:S(2)}) async-start(bf16[8,16,1024]{2,1,0:T(8,128)(2,1)} %pad_maximum_fusion), calls=%async_computation.6 | async-start | bytes 524288 | tf_op jit(solution)/shard_map/all_to_all | solution.py:34
  159.9 0.2 reduce_sum.25
  160.0 1.9 %collective-permute-start.4 = (bf16[80,512]{1,0:T(8,128)(2,1)S(1)}, bf16[80,512]{1,0:T(8,128)(2,1)S(1)}, u32[]{:S(2)}, u32[]{:S(2)}) collective-permute-start(bf16[80,512]{1,0:T(8,128)(2,1)S(1)} %reduce_sum.25), channel_id=1, source_target_pairs={{0,0},{4,1},{8,2},{12,3},{16,4},{20,5},{24,6},{28,7},{1,8},{5,9},{... | collective-permute-start | bytes 245768 | tf_op jit(solution)/shard_map/ppermute | solution.py:577
  162.0 4.4 %collective-permute-start.5 = (bf16[80,512]{1,0:T(8,128)(2,1)S(1)}, bf16[80,512]{1,0:T(8,128)(2,1)S(1)}, u32[]{:S(2)}, u32[]{:S(2)}) collective-permute-start(bf16[80,512]{1,0:T(8,128)(2,1)S(1)} %reduce_sum.25), channel_id=1, source_target_pairs={{0,64},{4,65},{8,66},{12,67},{16,68},{20,69},{24,70},{28,71},{1,72... | collective-permute-start | bytes 245768 | tf_op jit(solution)/shard_map/ppermute | solution.py:578
  166.4 0.0 reduce-scatter.3.cloned.1.call-done.norm_grad
  166.4 3.2 %shard_map.251 = (bf16[128,1024]{1,0:T(8,128)(2,1)}, f32[128,1024]{1,0:T(8,128)}) custom-call(s32[6]{0:T(128)} %stack.39.at, bf16[128,1024]{1,0:T(8,128)(2,1)} %tokens.3, bf16[128,1024]{1,0:T(8,128)(2,1)} %out_grad.1, bf16[128,1024]{1,0:T(8,128)(2,1)} %reduce-scatter.3.cloned.1.call-done.norm_grad, ...), custom_call_target="tpu_custom_call" | custom-call | bytes 1024 | tf_op jit(solution)/shard_map/pallas_call | solution.py:50
  169.6 0.0 collective-permute-done.4.refs_1_
  169.6 0.0 copy-start.4
  169.6 7.4 %collective-permute-done.5.refs_2_ = bf16[80,512]{1,0:T(8,128)(2,1)S(1)} collective-permute-done((bf16[80,512]{1,0:T(8,128)(2,1)S(1)}, bf16[80,512]{1,0:T(8,128)(2,1)S(1)}, u32[]{:S(2)}, u32[]{:S(2)}) %collective-permute-start.5) | collective-permute-done | bytes 81952 | tf_op jit(solution)/shard_map/ppermute | solution.py:578
  177.1 0.0 copy-start.5
  177.1 0.0 all-to-all-done.4.refs_0_
  177.1 0.0 copy-start.2
  177.1 0.0 copy-done.4
  177.1 0.6 copy-done.5
  177.7 0.1 copy-done.2
  177.8 2.0 %shard_map.252 = (f32[16,3072]{1,0:T(8,128)}, f32[16,4096]{1,0:T(8,128)}, f32[16]{0:T(128)}, f32[16]{0:T(128)}, f32[16]{0:T(128)}, /*index=5*/f32[16]{0:T(128)},...) custom-call(s32[6]{0:T(128)} %stack.39.at, ...), custom_call_target="tpu_custom_call" | custom-call | bytes 1024 | tf_op jit(solution)/shard_map/pallas_call | solution.py:50
  (6 shorter events, 0.1 us)
Async XLA Ops:
  7.2 63.0 %all-gather.5.cloned.1.call-start = ((), (), s32[]{:S(2)}) async-start(), calls=%async_computation.8 | async-start | bytes 2359296 | tf_op jit(solution)/shard_map/all_gather | solution.py:501
  12.4 71.2 %all-gather.3.cloned.1.call-start = ((), (), s32[]{:S(2)}) async-start(), calls=%async_computation.7 | async-start | bytes 2359296 | tf_op jit(solution)/shard_map/all_gather | solution.py:501
  14.0 3.5 %collective-permute-start.1 = (bf16[16,1024]{1,0:T(8,128)(2,1)S(1)}, bf16[16,1024]{1,0:T(8,128)(2,1)S(1)}, u32[]{:S(2)}, u32[]{:S(2)}) collective-permute-start(bf16[16,1024]{1,0:T(8,128)(2,1)S(1)} %get-tuple-element.82), channel_id=1, source_target_pairs={{0,32},{1,33},{32,0},{33,1},{2,34},{3,35},{34,2},{35,3},{4,36},{5,... | collective-permute-start | bytes 98312 | tf_op jit(solution)/shard_map/ppermute | solution.py:30
  16.2 3.7 %collective-permute-start.2 = (bf16[16,1024]{1,0:T(8,128)(2,1)S(1)}, bf16[16,1024]{1,0:T(8,128)(2,1)S(1)}, u32[]{:S(2)}, u32[]{:S(2)}) collective-permute-start(bf16[16,1024]{1,0:T(8,128)(2,1)S(1)} %get-tuple-element.81), channel_id=1, source_target_pairs={{0,33},{1,32},{32,1},{33,0},{2,35},{3,34},{34,3},{35,2},{4,37},{5,... | collective-permute-start | bytes 98312 | tf_op jit(solution)/shard_map/ppermute | solution.py:30
  17.1 2.8 %collective-permute-start = (bf16[16,1024]{1,0:T(8,128)(2,1)S(1)}, bf16[16,1024]{1,0:T(8,128)(2,1)S(1)}, u32[]{:S(2)}, u32[]{:S(2)}) collective-permute-start(bf16[16,1024]{1,0:T(8,128)(2,1)S(1)} %get-tuple-element.83), channel_id=1, source_target_pairs={{0,1},{1,0},{32,33},{33,32},{2,3},{3,2},{34,35},{35,34},{4,5},{5,4... | collective-permute-start | bytes 98312 | tf_op jit(solution)/shard_map/ppermute | solution.py:30
  21.6 7.7 %copy-start.3 = (bf16[64,1024]{1,0:T(8,128)(2,1)S(1)}, bf16[64,1024]{1,0:T(8,128)(2,1)}, u32[]{:S(2)}) copy-start(bf16[64,1024]{1,0:T(8,128)(2,1)} %param.25) | copy-start | bytes 393220
  21.6 7.8 %copy-start.6 = (bf16[16,1024]{1,0:T(8,128)(2,1)S(1)}, bf16[16,1024]{1,0:T(8,128)(2,1)}, u32[]{:S(2)}) copy-start(bf16[16,1024]{1,0:T(8,128)(2,1)} %param.21) | copy-start | bytes 98308
  21.6 38.3 %all-to-all-start = ((bf16[16,4,16,1024]{3,2,1,0:T(8,128)(2,1)}), bf16[16,4,16,1024]{3,2,1,0:T(8,128)(2,1)S(1)}, u32[]{:S(2)}, u32[]{:S(2)}) async-start(bf16[16,4,16,1024]{3,2,1,0:T(8,128)(2,1)} %broadcast_in_dim.41), calls=%async_computation | async-start | bytes 4194304 | tf_op jit(solution)/shard_map/all_to_all | solution.py:34
  29.4 27.5 %collective-permute-start.3 = (bf16[80,512]{1,0:T(8,128)(2,1)S(1)}, bf16[80,512]{1,0:T(8,128)(2,1)S(1)}, u32[]{:S(2)}, u32[]{:S(2)}) collective-permute-start(bf16[80,512]{1,0:T(8,128)(2,1)S(1)} %fusion.4), channel_id=1, source_target_pairs={{0,0},{1,4},{2,8},{3,12},{4,16},{5,20},{6,24},{7,28},{8,1},{9,5},{... | collective-permute-start | bytes 245768 | tf_op jit(solution)/shard_map/ppermute | solution.py:548
  59.8 10.4 %copy-start = (bf16[16,4,16,1024]{3,2,1,0:T(8,128)(2,1)}, bf16[16,4,16,1024]{3,2,1,0:T(8,128)(2,1)S(1)}, u32[]{:S(2)}) copy-start(bf16[16,4,16,1024]{3,2,1,0:T(8,128)(2,1)S(1)} %all-to-all-done.pieces) | copy-start | bytes 6291460
  61.2 27.1 %all-to-all-start.1 = ((bf16[16,80,512]{2,1,0:T(8,128)(2,1)}), bf16[16,80,512]{2,1,0:T(8,128)(2,1)S(1)}, u32[]{:S(2)}, u32[]{:S(2)}) async-start(bf16[16,80,512]{2,1,0:T(8,128)(2,1)} %broadcast_in_dim.47), calls=%async_computation.1 | async-start | bytes 2621440 | tf_op jit(solution)/shard_map/all_to_all | solution.py:34
  68.8 84.1 %reduce-scatter.5.cloned.1.call-start = ((), (), s32[]{:S(2)}) async-start(), calls=%async_computation.10 | async-start | bytes 2359296 | tf_op jit(solution)/shard_map/reduce_scatter | solution.py:505
  88.3 1.1 copy-start.1
  94.9 25.0 %all-to-all-start.2 = ((bf16[16,80,512]{2,1,0:T(8,128)(2,1)}), bf16[16,80,512]{2,1,0:T(8,128)(2,1)S(1)}, u32[]{:S(2)}, u32[]{:S(2)}) async-start(bf16[16,80,512]{2,1,0:T(8,128)(2,1)} %get-tuple-element.50.ahead.refs_13_), calls=%async_computation.2 | async-start | bytes 2621440 | tf_op jit(solution)/shard_map/all_to_all | solution.py:34
  101.6 64.8 %reduce-scatter.3.cloned.1.call-start = ((), (), s32[]{:S(2)}) async-start(), calls=%async_computation.9 | async-start | bytes 2359296 | tf_op jit(solution)/shard_map/reduce_scatter | solution.py:505
  153.6 23.4 %all-to-all-start.4 = ((bf16[8,16,1024]{2,1,0:T(8,128)(2,1)}), bf16[8,16,1024]{2,1,0:T(8,128)(2,1)S(1)}, u32[]{:S(2)}, u32[]{:S(2)}) async-start(bf16[8,16,1024]{2,1,0:T(8,128)(2,1)} %pad_maximum_fusion), calls=%async_computation.6 | async-start | bytes 524288 | tf_op jit(solution)/shard_map/all_to_all | solution.py:34
  160.0 9.6 %collective-permute-start.4 = (bf16[80,512]{1,0:T(8,128)(2,1)S(1)}, bf16[80,512]{1,0:T(8,128)(2,1)S(1)}, u32[]{:S(2)}, u32[]{:S(2)}) collective-permute-start(bf16[80,512]{1,0:T(8,128)(2,1)S(1)} %reduce_sum.25), channel_id=1, source_target_pairs={{0,0},{4,1},{8,2},{12,3},{16,4},{20,5},{24,6},{28,7},{1,8},{5,9},{... | collective-permute-start | bytes 245768 | tf_op jit(solution)/shard_map/ppermute | solution.py:577
  162.0 15.1 %collective-permute-start.5 = (bf16[80,512]{1,0:T(8,128)(2,1)S(1)}, bf16[80,512]{1,0:T(8,128)(2,1)S(1)}, u32[]{:S(2)}, u32[]{:S(2)}) collective-permute-start(bf16[80,512]{1,0:T(8,128)(2,1)S(1)} %reduce_sum.25), channel_id=1, source_target_pairs={{0,64},{4,65},{8,66},{12,67},{16,68},{20,69},{24,70},{28,71},{1,72... | collective-permute-start | bytes 245768 | tf_op jit(solution)/shard_map/ppermute | solution.py:578
  169.6 7.5 %copy-start.4 = (bf16[80,512]{1,0:T(8,128)(2,1)}, bf16[80,512]{1,0:T(8,128)(2,1)S(1)}, u32[]{:S(2)}) copy-start(bf16[80,512]{1,0:T(8,128)(2,1)S(1)} %collective-permute-done.4.refs_1_) | copy-start | bytes 245764
  177.1 0.6 copy-start.5
  177.1 0.7 copy-start.2
Sparse Core Ops, SparseCore 0:
  12.5 28.7 all-gather.4
  43.1 25.6 all-gather.2
  95.0 32.0 reduce-scatter.4
  129.4 32.4 reduce-scatter.2

commit v2 on v1

--- a/solution.py
+++ b/solution.py
@@ -306,13 +306,17 @@
     )(at, xh, pieces, *tables)
 
 
-def mixed_body(both, blocks, ahead, out_ref, turned, both_here, blocks_here, tail, buffer, done, written):
+def assemble(blocks, tail):
+    for place in range(16):
+        k, lane = place // 2, (place % 2) * 512
+        tail[k * 16 : k * 16 + 16, lane : lane + 512] = blocks[place, 0:16, :]
+        tail[128 + k * 64 : 192 + k * 64, lane : lane + 512] = blocks[place, 16:80, :]
+
+
+def mixed_body(both, blocks, ahead, out_ref, both_here, blocks_here, tail, buffer, done, written):
     started = fetch((blocks, both), (blocks_here, both_here), done)
     started[0].wait()
-    for place in range(16):
-        k, lane = place // 2, (place % 2) * 512
-        tail[k * 16 : k * 16 + 16, lane : lane + 512] = blocks_here[place, 0:16, :]
-        tail[128 + k * 64 : 192 + k * 64, lane : lane + 512] = blocks_here[place, 16:80, :]
+    assemble(blocks_here, tail)
     started[1].wait()
     stores = []
     for i in range(4):
@@ -320,7 +324,6 @@
         buffer[:, i] = product.astype(BF16).reshape(2, TOK, WIDTH)
         stores.append(pltpu.make_async_copy(buffer.at[:, i], out_ref.at[:, i], written.at[i]))
         stores[-1].start()
-    turned[...] = tail[...].T
     for copy in stores:
         copy.wait()
 
@@ -329,9 +332,9 @@
     remote = pl.BlockSpec(memory_space=pltpu.HBM)
     return pl.pallas_call(
         mixed_body,
-        out_shape=(token_shape(WIDTH, BF16), jax.ShapeDtypeStruct((WIDTH, 640), BF16)),
-        in_specs=[remote, remote, pl.BlockSpec(memory_space=pl.ANY)],
-        out_specs=(remote, vmem()),
+        out_shape=token_shape(WIDTH, BF16),
+        in_specs=[pl.BlockSpec(memory_space=pl.ANY)] * 3,
+        out_specs=remote,
         scratch_shapes=[
             pltpu.VMEM(both.shape, BF16),
             pltpu.VMEM(blocks.shape, BF16),
@@ -397,11 +400,13 @@
 
 def backward_body(at, *refs):
     sources, (norm_out, columns_out), copies = refs[:13], refs[15:17], refs[17:30]
-    grads, norm_buffer, columns_buffer, done, written = refs[30:]
-    cot, tail, rotated, sums, slope, cos, sin_low, sin_high, scaled, total, xh, columns, hot = copies
+    grads, norm_buffer, columns_buffer, weights, done, written = refs[30:]
+    cot, blocks, rotated, sums, slope, cos, sin_low, sin_high, scaled, total, xh, columns, hot = copies
     started = fetch(sources, copies, done)
     for copy in started[:8]:
         copy.wait()
+    assemble(blocks, weights)
+    tail = weights[...].T
     table = cos[...], sin_low[...], sin_high[...]
     stores = []
     for i in range(4):
@@ -447,13 +452,14 @@
     return pl.pallas_call(
         backward_body,
         out_shape=(token_shape(WIDTH, BF16), jax.ShapeDtypeStruct((16, 4, 16, WIDTH), BF16)),
-        in_specs=[smem()] + [remote] * 13 + [pl.BlockSpec(memory_space=pl.ANY)] * 2,
+        in_specs=[smem()] + [pl.BlockSpec(memory_space=pl.ANY)] * 15,
         out_specs=(remote, remote),
         scratch_shapes=[pltpu.VMEM(a.shape, a.dtype) for a in operands[:13]]
         + [
             pltpu.VMEM((2, 4, TOK, COLS), BF16),
             pltpu.VMEM((2, 4, TOK, WIDTH), BF16),
             pltpu.VMEM((16, 4, 16, WIDTH), BF16),
+            pltpu.VMEM((640, WIDTH), BF16),
             pltpu.SemaphoreType.DMA((13,)),
             pltpu.SemaphoreType.DMA((8,)),
         ],
@@ -556,17 +562,19 @@
     tables = rotary_tables()
     rotated, sums, both, slope, turned, columns_in, hot, flipped = forward(at, xh_tokens, pieces, tables)
     tail_grad, total = tail_grad_of(both.reshape(WIDTH, 640), cot)
-    mixed_part, tail = mixed_of(both, tail, tail_grad)
+    mixed_part = mixed_of(both, tail, tail_grad)
     tail_parts = spread(tail_grad, PLACES)
     mixed_sum = scatter_tokens(mixed_part.reshape(WIDTH, WIDTH))
     norm_part, columns_grad = backward(
-        at, cot_tokens, tail, rotated, sums, slope, *tables, turned, total, flipped, columns_in, hot, tail_grad, mixed_part
+        at, cot_tokens, tail, rotated, sums, slope, *tables, turned, total, flipped, columns_in, hot, tail_grad, tail_grad
     )
     norm_part, columns_grad = after((norm_part, columns_grad), tail_parts)
     norm_grad = scatter_tokens(norm_part.reshape(WIDTH, WIDTH))
+    column_sum = jnp.sum(spread(columns_grad, PLACES).astype(F32), axis=0).astype(BF16)
     tail_sum = jnp.sum(tail_parts.astype(F32), axis=0).astype(BF16)
-    column_sum = jnp.sum(spread(columns_grad, PLACES).astype(F32), axis=0).astype(BF16)
-    column_sum = after(column_sum, mixed_sum)
+    mine = lax.ppermute(tail_sum, AXES, [(b, a) for a, b in straight])
+    other = lax.ppermute(tail_sum, AXES, [(b, a) for a, b in crossed])
+    column_sum = after(column_sum, (mixed_sum, mine, other))
     parts = spread(jnp.concatenate([column_sum, column_sum], axis=0), GROUP)
     vector = shape((16,), F32)
     mixed, tokens_grad = call(
@@ -574,8 +582,6 @@
         (shape((TOK, WIDTH), BF16), shape((TOK, WIDTH), F32)),
         (at, tokens, out_grad, norm_grad, mixed_sum, columns_in),
     )
-    mine = lax.ppermute(tail_sum, AXES, [(b, a) for a, b in straight])
-    other = lax.ppermute(tail_sum, AXES, [(b, a) for a, b in crossed])
     qkv_grad, fc_in_grad, *vectors_grad, dense_grad, fc_out_grad = call(
         owner_body,
         (shape((16, 3 * WIDTH), F32), shape((16, FF), F32))

time: 188 us -> 185 us (0.984)
  blocking collectives: 32.5 us -> 0 us
  waiting for transfers between devices: 36.8 us -> 61.2 us
  starting transfers between devices: 43.9 us -> 50.2 us
    all_to_all x1 -> x0, blocking collectives: 32.5 us -> none  [spread(): return lax.all_to_all(blocks, axes, split_axis=0, concat_axis=0, tiled=True)]
    all_to_all x4 -> x5, waiting for transfers between devices: 4.28 us -> 22.7 us  [spread(): return lax.all_to_all(blocks, axes, split_axis=0, concat_axis=0, tiled=True)]
    reduce_scatter x2, waiting for transfers between devices: 0.02 us -> 5.72 us  [scatter_tokens(): return lax.psum_scatter(partial, GROUP, scatter_dimension=0, tiled=True)]
    all_to_all x4 -> x5, starting transfers between devices: 28.2 us -> 32.5 us  [spread(): return lax.all_to_all(blocks, axes, split_axis=0, concat_axis=0, tiled=True)]
    ppermute x1, waiting for transfers between devices: 0.01 us -> 3.65 us  [local(): mine = lax.ppermute(tail_sum, AXES, [(b, a) for a, b in straight])]
    ppermute x1, starting transfers between devices: 1.92 us -> 5.57 us  [local(): mine = lax.ppermute(tail_sum, AXES, [(b, a) for a, b in straight])]
    ppermute x1, waiting for transfers between devices: 7.45 us -> 4.01 us  [local(): other = lax.ppermute(tail_sum, AXES, [(b, a) for a, b in crossed])]
  transfers between devices with their start and end apart: 14 -> 15, of which waited for: 6 -> 9; matrix products, arithmetic and copies ran while one was open for 3% -> 4% of each run, Pallas kernels for 20% -> 21%
where the time goes in v2:
time: 185 us; the launch traced here: 183 us
  waiting for transfers between devices  61.2 us (33%)
  starting transfers between devices  50.2 us (27%)
  Pallas kernels  48.9 us (26%)
  between operations  14 us (8%)
  local copies, waits for them, and re-layouts  6.24 us (3%)
  other arithmetic  2.67 us (1%)
    all_to_all x5, starting transfers between devices, spread(): return lax.all_to_all(blocks, axes, split_axis=0, concat_axis=0, tiled=True)  32.5 us
    all_to_all x5, waiting for transfers between devices, spread(): return lax.all_to_all(blocks, axes, split_axis=0, concat_axis=0, tiled=True)  22.7 us
    ppermute x1, waiting for transfers between devices, local(): tail = lax.ppermute(tail, AXES, straight)  21.6 us
    pallas_call x1, Pallas kernels, backward(): pl.pallas_call(backward_body, out_shape=(token_shape(WIDTH, BF16), jax.Sh...  16.8 us
    pallas_call x1, Pallas kernels, forward(): pl.pallas_call(forward_body, grid=(4,), out_shape=(token_shape(QKV, BF16)...  13.4 us
    pallas_call x3, Pallas kernels, call(): pl.pallas_call(body, out_shape=out_shape, in_specs=[smem()] + [vmem()] *...  7.1 us
    ppermute x1, starting transfers between devices, local(): tail = lax.ppermute(tail, AXES, straight)  5.88 us
    reduce_scatter x2, waiting for transfers between devices, scatter_tokens(): return lax.psum_scatter(partial, GROUP, scatter_dimension=0, tiled=True)  5.72 us
  transfers between devices with their start and end apart: 15, of which 9 were waited for; matrix products, arithmetic and copies ran while one was open for 4% of the time, Pallas kernels for 21%

profile of v2, /device:TPU:1, one launch (start us, length us, event | category | flops | bytes accessed | tf_op | source)
XLA Modules:
  0.0 183.2 jit_solution(11365413753774552668)
XLA Ops:
  7.2 0.0 all-gather.5.cloned.1.call-start
  7.2 0.7 stack.39.at
  7.9 2.6 %shard_map.245.ahead = bf16[4,16,1024]{2,1,0:T(8,128)(2,1)} custom-call(s32[6]{0:T(128)} %stack.39.at, bf16[16]{0:T(256)(128)(2,1)} %refs_0_.1, bf16[16]{0:T(256)(128)(2,1)} %refs_1_.1, bf16[16]{0:T(256)(128)(2,1)} %refs_2_.1, bf16[16]{0:T(256)(128)(2,1)} %refs_3_.1, bf16[16]{0:T(256)(128)(2,1)} %refs_4_.1, bf16[16]{0:T(256)(128)(2,1)} %refs_5_.1, ...), custom_call_target="tpu_custom_call" | custom-call | tf_op jit(solution)/shard_map/pallas_call | solution.py:98
  10.5 1.9 %shard_map.246 = bf16[128,1024]{1,0:T(8,128)(2,1)} custom-call(s32[6]{0:T(128)} %stack.39.at, bf16[128,1024]{1,0:T(8,128)(2,1)} %tokens.3, bf16[4,16,1024]{2,1,0:T(8,128)(2,1)} %shard_map.245.ahead), custom_call_target="tpu_custom_call" | custom-call | bytes 1024 | tf_op jit(solution)/shard_map/pallas_call | solution.py:50
  12.4 0.0 all-gather.5.cloned.1.call-update
  12.4 0.0 all-gather.3.cloned.1.call-start
  12.5 0.7 all-gather.3.cloned.1.call-update
  13.2 0.8 fusion.9
  14.0 2.2 %collective-permute-start.2 = (bf16[16,1024]{1,0:T(8,128)(2,1)S(1)}, bf16[16,1024]{1,0:T(8,128)(2,1)S(1)}, u32[]{:S(2)}, u32[]{:S(2)}) collective-permute-start(bf16[16,1024]{1,0:T(8,128)(2,1)S(1)} %get-tuple-element.78), channel_id=1, source_target_pairs={{0,32},{1,33},{32,0},{33,1},{2,34},{3,35},{34,2},{35,3},{4,36},{5,... | collective-permute-start | bytes 98312 | tf_op jit(solution)/shard_map/ppermute | solution.py:30
  16.2 0.9 collective-permute-start.3
  17.2 0.0 collective-permute-start.1
  17.2 0.3 collective-permute-done.2
  17.5 2.4 %collective-permute-done.3 = bf16[16,1024]{1,0:T(8,128)(2,1)S(1)} collective-permute-done((bf16[16,1024]{1,0:T(8,128)(2,1)S(1)}, bf16[16,1024]{1,0:T(8,128)(2,1)S(1)}, u32[]{:S(2)}, u32[]{:S(2)}) %collective-permute-start.3) | collective-permute-done | bytes 32800 | tf_op jit(solution)/shard_map/ppermute | solution.py:30
  19.9 0.0 collective-permute-done.1
  20.0 1.6 broadcast_in_dim.42
  21.6 0.0 copy-start.3
  21.6 0.0 copy-start.6
  21.6 7.7 %all-to-all-start = ((bf16[16,4,16,1024]{3,2,1,0:T(8,128)(2,1)}), bf16[16,4,16,1024]{3,2,1,0:T(8,128)(2,1)S(1)}, u32[]{:S(2)}, u32[]{:S(2)}) async-start(bf16[16,4,16,1024]{3,2,1,0:T(8,128)(2,1)} %broadcast_in_dim.42), calls=%async_computation | async-start | bytes 4194304 | tf_op jit(solution)/shard_map/all_to_all | solution.py:34
  29.3 0.0 copy-done.3
  29.3 0.0 copy-done.6
  29.4 5.9 %collective-permute-start = (bf16[80,512]{1,0:T(8,128)(2,1)S(1)}, bf16[80,512]{1,0:T(8,128)(2,1)S(1)}, u32[]{:S(2)}, u32[]{:S(2)}) collective-permute-start(bf16[80,512]{1,0:T(8,128)(2,1)S(1)} %fusion.4), channel_id=1, source_target_pairs={{0,0},{1,4},{2,8},{3,12},{4,16},{5,20},{6,24},{7,28},{8,1},{9,5},{... | collective-permute-start | bytes 245768 | tf_op jit(solution)/shard_map/ppermute | solution.py:554
  35.3 21.6 %collective-permute-done = bf16[80,512]{1,0:T(8,128)(2,1)S(1)} collective-permute-done((bf16[80,512]{1,0:T(8,128)(2,1)S(1)}, bf16[80,512]{1,0:T(8,128)(2,1)S(1)}, u32[]{:S(2)}, u32[]{:S(2)}) %collective-permute-start) | collective-permute-done | bytes 81952 | tf_op jit(solution)/shard_map/ppermute | solution.py:554
  56.8 3.0 %all-to-all-done.pieces = bf16[16,4,16,1024]{3,2,1,0:T(8,128)(2,1)S(1)} async-done(((bf16[16,4,16,1024]{3,2,1,0:T(8,128)(2,1)}), bf16[16,4,16,1024]{3,2,1,0:T(8,128)(2,1)S(1)}, u32[]{:S(2)}, u32[]{:S(2)}) %all-to-all-start) | async-done | bytes 2097184 | tf_op jit(solution)/shard_map/all_to_all | solution.py:34
  59.8 0.0 copy-start.1
  59.9 1.4 broadcast_in_dim.41
  61.2 7.6 %all-to-all-start.1 = ((bf16[16,80,512]{2,1,0:T(8,128)(2,1)}), bf16[16,80,512]{2,1,0:T(8,128)(2,1)S(1)}, u32[]{:S(2)}, u32[]{:S(2)}) async-start(bf16[16,80,512]{2,1,0:T(8,128)(2,1)} %broadcast_in_dim.41), calls=%async_computation.1 | async-start | bytes 2621440 | tf_op jit(solution)/shard_map/all_to_all | solution.py:34
  68.8 0.0 reduce-scatter.5.cloned.1.call-start
  68.9 1.3 fusion
  70.2 0.0 copy-done.1
  70.2 0.0 all-gather.5.cloned.1.call-done
  70.2 13.4 %shard_map.247 = (bf16[2,4,128,384]{3,2,1,0:T(8,128)(2,1)}, f32[2,4,128,128]{3,2,1,0:T(8,128)}, bf16[2,4,128,640]{3,2,1,0:T(8,128)(2,1)}, bf16[2,4,128,512]{3,2,...) custom-call(s32[6]{0:T(128)} %stack.39.at, ...), custom_call_target="tpu_custom_call" | custom-call | flops 4194304 | bytes 8192 | tf_op jit(solution)/shard_map/pallas_call | solution.py:272
  83.6 0.0 all-gather.3.cloned.1.call-done.cot
  83.7 4.6 %shard_map.248 = (bf16[16,80,512]{2,1,0:T(8,128)(2,1)}, f32[8,1024]{1,0:T(8,128)}) custom-call(bf16[1024,640]{1,0:T(8,128)(2,1)} %bitcast.22, bf16[1024,1024]{1,0:T(8,128)(2,1)} %all-gather.3.cloned.1.call-done.cot), custom_call_target="tpu_custom_call" | custom-call | flops 2097152 | bytes 6144 | tf_op jit(solution)/shard_map/pallas_call | solution.py:481
  88.3 0.0 all-to-all-done.1.refs_1_.blocks
  88.3 0.0 copy-start
  88.3 1.1 copy-done
  89.4 4.4 %shard_map.250 = bf16[2,4,128,1024]{3,2,1,0:T(8,128)(2,1)} custom-call(bf16[2,4,128,640]{3,2,1,0:T(8,128)(2,1)} %get-tuple-element.51.both, bf16[16,80,512]{2,1,0:T(8,128)(2,1)} %copy-done, bf16[16,80,512]{2,1,0:T(8,128)(2,1)} %get-tuple-element.56.refs_13_.refs_14_.ahead), custom_call_target="tpu_custom_call" | custom-call | flops 2097152 | bytes 6144 | tf_op jit(solution)/shard_map/pallas_call | solution.py:333
  93.7 0.0 reduce-scatter.5.cloned.1.call-update
  93.8 6.7 %all-to-all-start.2 = ((bf16[16,80,512]{2,1,0:T(8,128)(2,1)}), bf16[16,80,512]{2,1,0:T(8,128)(2,1)S(1)}, u32[]{:S(2)}, u32[]{:S(2)}) async-start(bf16[16,80,512]{2,1,0:T(8,128)(2,1)} %get-tuple-element.56.refs_13_.refs_14_.ahead), calls=%async_computation.2 | async-start | bytes 2621440 | tf_op jit(solution)/shard_map/all_to_all | solution.py:34
  100.4 0.2 reduce-scatter.3.cloned.1.call-start
  100.7 16.8 %shard_map.249 = (bf16[2,4,128,1024]{3,2,1,0:T(8,128)(2,1)}, bf16[16,4,16,1024]{3,2,1,0:T(8,128)(2,1)}) custom-call(s32[6]{0:T(128)} %stack.39.at, bf16[2,4,128,1024]{3,2,1,0:T(8,128)(2,1)} %bitcast.21, bf16[16,80,512]{2,1,0:T(8,128)(2,1)} %copy-done, bf16[2,4,128,384]{3,2,1,0:T(8,128)(2,1)} %get-tuple-element.47.refs_2_, ...), custom_call_target="tpu_custom_call" | custom-call | flops 6291456 | bytes 16384 | tf_op jit(solution)/shard_map/pallas_call | solution.py:452
  117.5 1.3 all-to-all-done.2
  118.8 0.0 reduce-scatter.3.cloned.1.call-update
  118.8 5.3 %all-to-all-start.3 = ((bf16[16,4,16,1024]{3,2,1,0:T(8,128)(2,1)}), bf16[16,4,16,1024]{3,2,1,0:T(8,128)(2,1)S(1)}, u32[]{:S(2)}, u32[]{:S(2)}) async-start(bf16[16,4,16,1024]{3,2,1,0:T(8,128)(2,1)} %get-tuple-element.62), calls=%async_computation.5 | async-start | bytes 4194304 | tf_op jit(solution)/shard_map/all_to_all | solution.py:34
  124.1 0.2 reduce_sum.25
  124.3 5.6 %collective-permute-start.4 = (bf16[80,512]{1,0:T(8,128)(2,1)S(1)}, bf16[80,512]{1,0:T(8,128)(2,1)S(1)}, u32[]{:S(2)}, u32[]{:S(2)}) collective-permute-start(bf16[80,512]{1,0:T(8,128)(2,1)S(1)} %reduce_sum.25), channel_id=1, source_target_pairs={{0,0},{4,1},{8,2},{12,3},{16,4},{20,5},{24,6},{28,7},{1,8},{5,9},{... | collective-permute-start | bytes 245768 | tf_op jit(solution)/shard_map/ppermute | solution.py:575
  129.8 2.8 %collective-permute-start.5 = (bf16[80,512]{1,0:T(8,128)(2,1)S(1)}, bf16[80,512]{1,0:T(8,128)(2,1)S(1)}, u32[]{:S(2)}, u32[]{:S(2)}) collective-permute-start(bf16[80,512]{1,0:T(8,128)(2,1)S(1)} %reduce_sum.25), channel_id=1, source_target_pairs={{0,64},{4,65},{8,66},{12,67},{16,68},{20,69},{24,70},{28,71},{1,72... | collective-permute-start | bytes 245768 | tf_op jit(solution)/shard_map/ppermute | solution.py:576
  132.6 18.3 %all-to-all-done.3 = bf16[16,4,16,1024]{3,2,1,0:T(8,128)(2,1)S(1)} async-done(((bf16[16,4,16,1024]{3,2,1,0:T(8,128)(2,1)}), bf16[16,4,16,1024]{3,2,1,0:T(8,128)(2,1)S(1)}, u32[]{:S(2)}, u32[]{:S(2)}) %all-to-all-start.3) | async-done | bytes 2097184 | tf_op jit(solution)/shard_map/all_to_all | solution.py:34
  150.9 0.4 reduce_sum.24
  151.3 3.7 %collective-permute-done.4.refs_1_ = bf16[80,512]{1,0:T(8,128)(2,1)S(1)} collective-permute-done((bf16[80,512]{1,0:T(8,128)(2,1)S(1)}, bf16[80,512]{1,0:T(8,128)(2,1)S(1)}, u32[]{:S(2)}, u32[]{:S(2)}) %collective-permute-start.4) | collective-permute-done | bytes 81952 | tf_op jit(solution)/shard_map/ppermute | solution.py:575
  155.0 0.0 copy-start.4
  155.0 4.0 %collective-permute-done.5.refs_2_ = bf16[80,512]{1,0:T(8,128)(2,1)S(1)} collective-permute-done((bf16[80,512]{1,0:T(8,128)(2,1)S(1)}, bf16[80,512]{1,0:T(8,128)(2,1)S(1)}, u32[]{:S(2)}, u32[]{:S(2)}) %collective-permute-start.5) | collective-permute-done | bytes 81952 | tf_op jit(solution)/shard_map/ppermute | solution.py:576
  159.0 0.0 copy-start.5
  159.0 0.0 reduce-scatter.5.cloned.1.call-done.mixed_sum
  159.0 0.7 pad_maximum_fusion
  159.7 5.3 %all-to-all-start.4 = ((bf16[8,16,1024]{2,1,0:T(8,128)(2,1)}), bf16[8,16,1024]{2,1,0:T(8,128)(2,1)S(1)}, u32[]{:S(2)}, u32[]{:S(2)}) async-start(bf16[8,16,1024]{2,1,0:T(8,128)(2,1)} %pad_maximum_fusion), calls=%async_computation.6 | async-start | bytes 524288 | tf_op jit(solution)/shard_map/all_to_all | solution.py:34
  165.0 5.7 %reduce-scatter.3.cloned.1.call-done.norm_grad = bf16[128,1024]{1,0:T(8,128)(2,1)} async-done(((bf16[1024,1024]{1,0:T(8,128)(2,1)}), bf16[128,1024]{1,0:T(8,128)(2,1)}) %reduce-scatter.3.cloned.1.call-update) | async-done | bytes 262160 | tf_op jit(solution)/shard_map/reduce_scatter | solution.py:511
  170.7 3.2 %shard_map.251 = (bf16[128,1024]{1,0:T(8,128)(2,1)}, f32[128,1024]{1,0:T(8,128)}) custom-call(s32[6]{0:T(128)} %stack.39.at, bf16[128,1024]{1,0:T(8,128)(2,1)} %tokens.3, bf16[128,1024]{1,0:T(8,128)(2,1)} %out_grad.1, bf16[128,1024]{1,0:T(8,128)(2,1)} %reduce-scatter.3.cloned.1.call-done.norm_grad, ...), custom_call_target="tpu_custom_call" | custom-call | bytes 1024 | tf_op jit(solution)/shard_map/pallas_call | solution.py:50
  174.0 0.0 all-to-all-done.4.refs_0_
  174.0 0.0 copy-start.2
  174.0 0.0 copy-done.4
  174.0 0.0 copy-done.5
  174.0 0.7 copy-done.2
  174.7 2.0 %shard_map.252 = (f32[16,3072]{1,0:T(8,128)}, f32[16,4096]{1,0:T(8,128)}, f32[16]{0:T(128)}, f32[16]{0:T(128)}, f32[16]{0:T(128)}, /*index=5*/f32[16]{0:T(128)},...) custom-call(s32[6]{0:T(128)} %stack.39.at, ...), custom_call_target="tpu_custom_call" | custom-call | bytes 1024 | tf_op jit(solution)/shard_map/pallas_call | solution.py:50
  (6 shorter events, 0.1 us)
Async XLA Ops:
  7.2 63.0 %all-gather.5.cloned.1.call-start = ((), (), s32[]{:S(2)}) async-start(), calls=%async_computation.8 | async-start | bytes 2359296 | tf_op jit(solution)/shard_map/all_gather | solution.py:507
  12.4 71.2 %all-gather.3.cloned.1.call-start = ((), (), s32[]{:S(2)}) async-start(), calls=%async_computation.7 | async-start | bytes 2359296 | tf_op jit(solution)/shard_map/all_gather | solution.py:507
  14.0 3.5 %collective-permute-start.2 = (bf16[16,1024]{1,0:T(8,128)(2,1)S(1)}, bf16[16,1024]{1,0:T(8,128)(2,1)S(1)}, u32[]{:S(2)}, u32[]{:S(2)}) collective-permute-start(bf16[16,1024]{1,0:T(8,128)(2,1)S(1)} %get-tuple-element.78), channel_id=1, source_target_pairs={{0,32},{1,33},{32,0},{33,1},{2,34},{3,35},{34,2},{35,3},{4,36},{5,... | collective-permute-start | bytes 98312 | tf_op jit(solution)/shard_map/ppermute | solution.py:30
  16.2 3.7 %collective-permute-start.3 = (bf16[16,1024]{1,0:T(8,128)(2,1)S(1)}, bf16[16,1024]{1,0:T(8,128)(2,1)S(1)}, u32[]{:S(2)}, u32[]{:S(2)}) collective-permute-start(bf16[16,1024]{1,0:T(8,128)(2,1)S(1)} %get-tuple-element.77), channel_id=1, source_target_pairs={{0,33},{1,32},{32,1},{33,0},{2,35},{3,34},{34,3},{35,2},{4,37},{5,... | collective-permute-start | bytes 98312 | tf_op jit(solution)/shard_map/ppermute | solution.py:30
  17.2 2.8 %collective-permute-start.1 = (bf16[16,1024]{1,0:T(8,128)(2,1)S(1)}, bf16[16,1024]{1,0:T(8,128)(2,1)S(1)}, u32[]{:S(2)}, u32[]{:S(2)}) collective-permute-start(bf16[16,1024]{1,0:T(8,128)(2,1)S(1)} %get-tuple-element.79), channel_id=1, source_target_pairs={{0,1},{1,0},{32,33},{33,32},{2,3},{3,2},{34,35},{35,34},{4,5},{5,4... | collective-permute-start | bytes 98312 | tf_op jit(solution)/shard_map/ppermute | solution.py:30
  21.6 7.7 %copy-start.3 = (bf16[64,1024]{1,0:T(8,128)(2,1)S(1)}, bf16[64,1024]{1,0:T(8,128)(2,1)}, u32[]{:S(2)}) copy-start(bf16[64,1024]{1,0:T(8,128)(2,1)} %param.25) | copy-start | bytes 393220
  21.6 7.8 %copy-start.6 = (bf16[16,1024]{1,0:T(8,128)(2,1)S(1)}, bf16[16,1024]{1,0:T(8,128)(2,1)}, u32[]{:S(2)}) copy-start(bf16[16,1024]{1,0:T(8,128)(2,1)} %param.21) | copy-start | bytes 98308
  21.6 38.3 %all-to-all-start = ((bf16[16,4,16,1024]{3,2,1,0:T(8,128)(2,1)}), bf16[16,4,16,1024]{3,2,1,0:T(8,128)(2,1)S(1)}, u32[]{:S(2)}, u32[]{:S(2)}) async-start(bf16[16,4,16,1024]{3,2,1,0:T(8,128)(2,1)} %broadcast_in_dim.42), calls=%async_computation | async-start | bytes 4194304 | tf_op jit(solution)/shard_map/all_to_all | solution.py:34
  29.4 27.5 %collective-permute-start = (bf16[80,512]{1,0:T(8,128)(2,1)S(1)}, bf16[80,512]{1,0:T(8,128)(2,1)S(1)}, u32[]{:S(2)}, u32[]{:S(2)}) collective-permute-start(bf16[80,512]{1,0:T(8,128)(2,1)S(1)} %fusion.4), channel_id=1, source_target_pairs={{0,0},{1,4},{2,8},{3,12},{4,16},{5,20},{6,24},{7,28},{8,1},{9,5},{... | collective-permute-start | bytes 245768 | tf_op jit(solution)/shard_map/ppermute | solution.py:554
  59.8 10.4 %copy-start.1 = (bf16[16,4,16,1024]{3,2,1,0:T(8,128)(2,1)}, bf16[16,4,16,1024]{3,2,1,0:T(8,128)(2,1)S(1)}, u32[]{:S(2)}) copy-start(bf16[16,4,16,1024]{3,2,1,0:T(8,128)(2,1)S(1)} %all-to-all-done.pieces) | copy-start | bytes 6291460
  61.2 27.1 %all-to-all-start.1 = ((bf16[16,80,512]{2,1,0:T(8,128)(2,1)}), bf16[16,80,512]{2,1,0:T(8,128)(2,1)S(1)}, u32[]{:S(2)}, u32[]{:S(2)}) async-start(bf16[16,80,512]{2,1,0:T(8,128)(2,1)} %broadcast_in_dim.41), calls=%async_computation.1 | async-start | bytes 2621440 | tf_op jit(solution)/shard_map/all_to_all | solution.py:34
  68.8 90.2 %reduce-scatter.5.cloned.1.call-start = ((), (), s32[]{:S(2)}) async-start(), calls=%async_computation.10 | async-start | bytes 2359296 | tf_op jit(solution)/shard_map/reduce_scatter | solution.py:511
  88.3 1.1 copy-start
  93.8 25.0 %all-to-all-start.2 = ((bf16[16,80,512]{2,1,0:T(8,128)(2,1)}), bf16[16,80,512]{2,1,0:T(8,128)(2,1)S(1)}, u32[]{:S(2)}, u32[]{:S(2)}) async-start(bf16[16,80,512]{2,1,0:T(8,128)(2,1)} %get-tuple-element.56.refs_13_.refs_14_.ahead), calls=%async_computation.2 | async-start | bytes 2621440 | tf_op jit(solution)/shard_map/all_to_all | solution.py:34
  100.4 70.3 %reduce-scatter.3.cloned.1.call-start = ((), (), s32[]{:S(2)}) async-start(), calls=%async_computation.9 | async-start | bytes 2359296 | tf_op jit(solution)/shard_map/reduce_scatter | solution.py:511
  118.8 32.1 %all-to-all-start.3 = ((bf16[16,4,16,1024]{3,2,1,0:T(8,128)(2,1)}), bf16[16,4,16,1024]{3,2,1,0:T(8,128)(2,1)S(1)}, u32[]{:S(2)}, u32[]{:S(2)}) async-start(bf16[16,4,16,1024]{3,2,1,0:T(8,128)(2,1)} %get-tuple-element.62), calls=%async_computation.5 | async-start | bytes 4194304 | tf_op jit(solution)/shard_map/all_to_all | solution.py:34
  124.3 30.7 %collective-permute-start.4 = (bf16[80,512]{1,0:T(8,128)(2,1)S(1)}, bf16[80,512]{1,0:T(8,128)(2,1)S(1)}, u32[]{:S(2)}, u32[]{:S(2)}) collective-permute-start(bf16[80,512]{1,0:T(8,128)(2,1)S(1)} %reduce_sum.25), channel_id=1, source_target_pairs={{0,0},{4,1},{8,2},{12,3},{16,4},{20,5},{24,6},{28,7},{1,8},{5,9},{... | collective-permute-start | bytes 245768 | tf_op jit(solution)/shard_map/ppermute | solution.py:575
  129.8 29.2 %collective-permute-start.5 = (bf16[80,512]{1,0:T(8,128)(2,1)S(1)}, bf16[80,512]{1,0:T(8,128)(2,1)S(1)}, u32[]{:S(2)}, u32[]{:S(2)}) collective-permute-start(bf16[80,512]{1,0:T(8,128)(2,1)S(1)} %reduce_sum.25), channel_id=1, source_target_pairs={{0,64},{4,65},{8,66},{12,67},{16,68},{20,69},{24,70},{28,71},{1,72... | collective-permute-start | bytes 245768 | tf_op jit(solution)/shard_map/ppermute | solution.py:576
  155.0 19.0 %copy-start.4 = (bf16[80,512]{1,0:T(8,128)(2,1)}, bf16[80,512]{1,0:T(8,128)(2,1)S(1)}, u32[]{:S(2)}) copy-start(bf16[80,512]{1,0:T(8,128)(2,1)S(1)} %collective-permute-done.4.refs_1_) | copy-start | bytes 245764
  159.0 15.0 %copy-start.5 = (bf16[80,512]{1,0:T(8,128)(2,1)}, bf16[80,512]{1,0:T(8,128)(2,1)S(1)}, u32[]{:S(2)}) copy-start(bf16[80,512]{1,0:T(8,128)(2,1)S(1)} %collective-permute-done.5.refs_2_) | copy-start | bytes 245764
  159.7 14.2 %all-to-all-start.4 = ((bf16[8,16,1024]{2,1,0:T(8,128)(2,1)}), bf16[8,16,1024]{2,1,0:T(8,128)(2,1)S(1)}, u32[]{:S(2)}, u32[]{:S(2)}) async-start(bf16[8,16,1024]{2,1,0:T(8,128)(2,1)} %pad_maximum_fusion), calls=%async_computation.6 | async-start | bytes 524288 | tf_op jit(solution)/shard_map/all_to_all | solution.py:34
  174.0 0.7 copy-start.2
Sparse Core Ops, SparseCore 0:
  12.6 28.7 all-gather.4
  43.1 25.6 all-gather.2
  93.9 32.1 reduce-scatter.4
  128.3 42.3 reduce-scatter.2

commit v3 on v2

--- a/solution.py
+++ b/solution.py
@@ -81,23 +81,25 @@
     for vector, count in zip(copies, COUNTS):
         columns += columns_of(vector, count)
     for index, column in enumerate(columns):
-        small = jnp.where(lane == index, column, small)
+        small = jnp.where(lane == index + 32 * (at[1] * 2 + at[4]), column, small)
     small = small.astype(BF16)
     for d in range(4):
         rank = lax.bitwise_xor(at[5], d)
-        parts = []
-        for part in range(3):
-            first = pl.multiple_of(part * WIDTH + rank * 128, 128)
-            parts.append(qkv[:, pl.ds(first, 128)])
-        parts += [small, fc_in[:, pl.ds(pl.multiple_of(rank * HID, HID), HID)]]
-        out[d] = jnp.concatenate(parts, axis=1)
+        for j in range(7):
+            if j < 3:
+                first = pl.multiple_of(j * WIDTH + rank * 128, 128)
+                out[d, j * 16 : j * 16 + 16] = qkv[:, pl.ds(first, 128)]
+            else:
+                first = pl.multiple_of(rank * HID + (j - 3) * 128, 128)
+                out[d, j * 16 : j * 16 + 16] = fc_in[:, pl.ds(first, 128)]
+        out[d, 112:128] = small
 
 
 def pack(at, qkv_weight, fc_in_weight, vectors):
     anywhere = pl.BlockSpec(memory_space=pltpu.HBM)
     return pl.pallas_call(
         pack_body,
-        out_shape=jax.ShapeDtypeStruct((4, 16, WIDTH), BF16),
+        out_shape=jax.ShapeDtypeStruct((4, 128, 128), BF16),
         in_specs=[smem()] + [anywhere] * 10,
         out_specs=vmem(),
         scratch_shapes=[pltpu.VMEM((16 * count,), BF16) for count in COUNTS]
@@ -142,9 +144,12 @@
         block = pieces[rank]
         for part in range(3):
             first = part * WIDTH + rank * 128
-            qkv_out[:, first : first + 128] = block[:, part * 128 : part * 128 + 128].astype(F32)
-        small = small + block[:, QKV:512].astype(F32)
-        in_out[:, rank * HID : rank * HID + HID] = block[:, 512:].astype(F32)
+            qkv_out[:, first : first + 128] = block[part * 16 : part * 16 + 16].astype(F32)
+        small = small + block[112:128].astype(F32)
+        for j in range(3, 7):
+            first = rank * HID + (j - 3) * 128
+            in_out[:, first : first + 128] = block[j * 16 : j * 16 + 16].astype(F32)
+    small = pltpu.roll(small, lax.rem(128 - 32 * (at[1] * 2 + at[4]), 128), 1)
     lane = 0
     for vector, count in ((g1, 1), (b1, 1), (g2, 1), (b2, 1), (bias, 1), (None, 1), (qb, 3), (fb, 4)):
         if vector is not None:
@@ -195,6 +200,10 @@
     return row >= lax.broadcasted_iota(jnp.int32, (256, 256), 1)
 
 
+def lane_of(j):
+    return j * 128 if j < 3 else j * 128 + 128
+
+
 def owner_rows(at, place, d):
     pair = lax.bitwise_xor(at[1] * 2 + at[4], d)
     return pl.multiple_of((lax.shift_right_logical(pair, 1) * 16 + place) * 32 + lax.bitwise_and(pair, 1) * 16, 16)
@@ -207,7 +216,14 @@
     def _():
         for place in range(16):
             for d in range(4):
-                columns[pl.ds(owner_rows(at, place, d), 16), :] = pieces[place, d]
+                rows = pl.ds(owner_rows(at, place, d), 16)
+                for j in range(7):
+                    columns[rows, lane_of(j) : lane_of(j) + 128] = pieces[place, d * 112 + j * 16 : d * 112 + j * 16 + 16]
+            folded = pieces[place, 448:464].astype(F32)
+            for pair in range(4):
+                first = ((pair // 2) * 16 + place) * 32 + (pair % 2) * 16
+                own = pltpu.roll(folded, 128 - 32 * pair, 1) if pair else folded
+                columns[first : first + 16, QKV:512] = own.astype(BF16)
         params = columns[:, QKV:512]
         weights = jnp.concatenate([columns[:, :QKV], columns[:, 512:]], axis=1)
         row, lane = bias_places(rank, (WIDTH, COLS), 1)
@@ -285,7 +301,7 @@
         in_specs=[
             smem(),
             token_spec(WIDTH),
-            pl.BlockSpec((16, 4, 16, WIDTH), lambda i: (0, 0, 0, 0)),
+            pl.BlockSpec((16, 464, 128), lambda i: (0, 0, 0)),
             table,
             table,
             table,
@@ -439,10 +455,20 @@
         )
         place, pair = (block % 2) * 8, (block // 2) * 2
         for inside in range(16):
-            columns_buffer[place + inside // 2, pair + inside % 2] = result[inside * 16 : inside * 16 + 16]
-        here = (slice(place, place + 8), slice(pair, pair + 2))
-        stores.append(pltpu.make_async_copy(columns_buffer.at[here], columns_out.at[here], written.at[4 + block]))
-        stores[-1].start()
+            rows = slice(inside * 16, inside * 16 + 16)
+            here, owner = place + inside // 2, pair + inside % 2
+            for j in range(7):
+                first = owner * 112 + j * 16
+                columns_buffer[here, first : first + 16] = result[rows, lane_of(j) : lane_of(j) + 128]
+            own = result[rows, QKV:512].astype(F32)
+            own = pltpu.roll(own, 32 * owner, 1) if owner else own
+            if owner:
+                own = own + columns_buffer[here, 448:464].astype(F32)
+            columns_buffer[here, 448:464] = own.astype(BF16)
+        if block >= 2:
+            here = slice(place, place + 8)
+            stores.append(pltpu.make_async_copy(columns_buffer.at[here], columns_out.at[here], written.at[2 + block]))
+            stores[-1].start()
     for copy in stores:
         copy.wait()
 
@@ -451,17 +477,17 @@
     remote = pl.BlockSpec(memory_space=pltpu.HBM)
     return pl.pallas_call(
         backward_body,
-        out_shape=(token_shape(WIDTH, BF16), jax.ShapeDtypeStruct((16, 4, 16, WIDTH), BF16)),
+        out_shape=(token_shape(WIDTH, BF16), jax.ShapeDtypeStruct((16, 464, 128), BF16)),
         in_specs=[smem()] + [pl.BlockSpec(memory_space=pl.ANY)] * 15,
         out_specs=(remote, remote),
         scratch_shapes=[pltpu.VMEM(a.shape, a.dtype) for a in operands[:13]]
         + [
             pltpu.VMEM((2, 4, TOK, COLS), BF16),
             pltpu.VMEM((2, 4, TOK, WIDTH), BF16),
-            pltpu.VMEM((16, 4, 16, WIDTH), BF16),
+            pltpu.VMEM((16, 464, 128), BF16),
             pltpu.VMEM((640, WIDTH), BF16),
             pltpu.SemaphoreType.DMA((13,)),
-            pltpu.SemaphoreType.DMA((8,)),
+            pltpu.SemaphoreType.DMA((6,)),
         ],
         compiler_params=pltpu.CompilerParams(vmem_limit_bytes=VMEM_LIMIT),
         cost_estimate=cost(6 << 30, 16 << 20),
@@ -548,7 +574,9 @@
     vectors = (ln1_gain, ln1_bias, ln2_gain, ln2_bias, dense_bias, fc_out_bias, qkv_bias, fc_in_bias)
     sent = pack(at, qkv_weight, fc_in_weight, vectors)
     pieces = jnp.stack([sent[0]] + [exchange(sent[d], PAIR, 4, d) for d in range(1, 4)])
-    pieces = spread(jnp.broadcast_to(pieces, (16, 4, 16, WIDTH)), PLACES)
+    folded = pieces[0, 112:] + pieces[1, 112:] + pieces[2, 112:] + pieces[3, 112:]
+    pieces = jnp.concatenate([pieces[:, :112].reshape(448, 128), folded], axis=0)
+    pieces = spread(jnp.broadcast_to(pieces, (16, 464, 128)), PLACES)
     tail = jnp.concatenate([dense_weight, fc_out_weight], axis=0)
     tail = lax.dynamic_slice_in_dim(tail, s * 512, 512, axis=1)
     tail = lax.ppermute(tail, AXES, straight)
@@ -575,6 +603,8 @@
     mine = lax.ppermute(tail_sum, AXES, [(b, a) for a, b in straight])
     other = lax.ppermute(tail_sum, AXES, [(b, a) for a, b in crossed])
     column_sum = after(column_sum, (mixed_sum, mine, other))
+    small_sum = jnp.broadcast_to(column_sum[448:], (4, 16, 128))
+    column_sum = jnp.concatenate([column_sum[:448].reshape(4, 112, 128), small_sum], axis=1)
     parts = spread(jnp.concatenate([column_sum, column_sum], axis=0), GROUP)
     vector = shape((16,), F32)
     mixed, tokens_grad = call(

time: 185 us -> 182 us (0.984)
  waiting for transfers between devices: 61.2 us -> 58.1 us
    ppermute x1, waiting for transfers between devices: 21.6 us -> 18.7 us  [local(): tail = lax.ppermute(tail, AXES, straight)]
    all_to_all x5, waiting for transfers between devices: 22.7 us -> 20 us  [spread(): return lax.all_to_all(blocks, axes, split_axis=0, concat_axis=0, tiled=True)]
    reduce_scatter x2, waiting for transfers between devices: 5.72 us -> 8.25 us  [scatter_tokens(): return lax.psum_scatter(partial, GROUP, scatter_dimension=0, tiled=True)]
where the time goes in v3:
time: 182 us; the launch traced here: 181 us
  waiting for transfers between devices  58.1 us (32%)
  starting transfers between devices  50.1 us (28%)
  Pallas kernels  49.2 us (27%)
  between operations  14 us (8%)
  local copies, waits for them, and re-layouts  6.54 us (4%)
  other arithmetic  3.24 us (2%)
    all_to_all x5, starting transfers between devices, spread(): return lax.all_to_all(blocks, axes, split_axis=0, concat_axis=0, tiled=True)  32.5 us
    all_to_all x5, waiting for transfers between devices, spread(): return lax.all_to_all(blocks, axes, split_axis=0, concat_axis=0, tiled=True)  20 us
    ppermute x1, waiting for transfers between devices, local(): tail = lax.ppermute(tail, AXES, straight)  18.7 us
    pallas_call x1, Pallas kernels, backward(): pl.pallas_call(backward_body, out_shape=(token_shape(WIDTH, BF16), jax.Sh...  16.8 us
    pallas_call x1, Pallas kernels, forward(): pl.pallas_call(forward_body, grid=(4,), out_shape=(token_shape(QKV, BF16)...  13.6 us
    reduce_scatter x2, waiting for transfers between devices, scatter_tokens(): return lax.psum_scatter(partial, GROUP, scatter_dimension=0, tiled=True)  8.25 us
    pallas_call x3, Pallas kernels, call(): pl.pallas_call(body, out_shape=out_shape, in_specs=[smem()] + [vmem()] *...  7.17 us
    ppermute x1, starting transfers between devices, local(): tail = lax.ppermute(tail, AXES, straight)  5.88 us
  transfers between devices with their start and end apart: 15, of which 9 were waited for; matrix products, arithmetic and copies ran while one was open for 4% of the time, Pallas kernels for 21%

profile of v3, /device:TPU:1, one launch (start us, length us, event | category | flops | bytes accessed | tf_op | source)
XLA Modules:
  0.0 181.2 jit_solution(9364571945428218486)
XLA Ops:
  7.2 0.0 all-gather.5.cloned.1.call-start
  7.2 0.7 stack.39.at
  7.9 2.6 %shard_map.245.ahead = bf16[4,128,128]{2,1,0:T(8,128)(2,1)} custom-call(s32[6]{0:T(128)} %stack.39.at, bf16[16]{0:T(256)(128)(2,1)} %refs_0_.1, bf16[16]{0:T(256)(128)(2,1)} %refs_1_.1, bf16[16]{0:T(256)(128)(2,1)} %refs_2_.1, bf16[16]{0:T(256)(128)(2,1)} %refs_3_.1, bf16[16]{0:T(256)(128)(2,1)} %refs_4_.1, bf16[16]{0:T(256)(128)(2,1)} %refs_5_.1, ...), custom_call_target="tpu_custom_call" | custom-call | tf_op jit(solution)/shard_map/pallas_call | solution.py:100
  10.5 1.9 %shard_map.246 = bf16[128,1024]{1,0:T(8,128)(2,1)} custom-call(s32[6]{0:T(128)} %stack.39.at, bf16[128,1024]{1,0:T(8,128)(2,1)} %tokens.3, bf16[4,128,128]{2,1,0:T(8,128)(2,1)} %shard_map.245.ahead), custom_call_target="tpu_custom_call" | custom-call | bytes 1024 | tf_op jit(solution)/shard_map/pallas_call | solution.py:50
  12.4 0.0 all-gather.5.cloned.1.call-update
  12.4 0.0 all-gather.3.cloned.1.call-start
  12.5 0.7 all-gather.3.cloned.1.call-update
  13.2 0.8 fusion.10
  14.0 2.2 %collective-permute-start.2 = (bf16[128,128]{1,0:T(8,128)(2,1)S(1)}, bf16[128,128]{1,0:T(8,128)(2,1)S(1)}, u32[]{:S(2)}, u32[]{:S(2)}) collective-permute-start(bf16[128,128]{1,0:T(8,128)(2,1)S(1)} %get-tuple-element.78), channel_id=1, source_target_pairs={{0,32},{1,33},{32,0},{33,1},{2,34},{3,35},{34,2},{35,3},{4,36},{5,... | collective-permute-start | bytes 98312 | tf_op jit(solution)/shard_map/ppermute | solution.py:30
  16.2 0.9 collective-permute-start.3
  17.2 0.0 collective-permute-start.1
  17.2 0.3 collective-permute-done.2
  17.5 2.4 %collective-permute-done.3 = bf16[128,128]{1,0:T(8,128)(2,1)S(1)} collective-permute-done((bf16[128,128]{1,0:T(8,128)(2,1)S(1)}, bf16[128,128]{1,0:T(8,128)(2,1)S(1)}, u32[]{:S(2)}, u32[]{:S(2)}) %collective-permute-start.3) | collective-permute-done | bytes 32800 | tf_op jit(solution)/shard_map/ppermute | solution.py:30
  19.9 0.0 collective-permute-done.1
  20.0 0.7 fusion.5
  20.7 1.5 broadcast_in_dim.45
  22.2 0.0 copy-start.3
  22.2 0.0 copy-start.6
  22.2 7.7 %all-to-all-start = ((bf16[16,464,128]{2,1,0:T(8,128)(2,1)}), bf16[16,464,128]{2,1,0:T(8,128)(2,1)S(1)}, u32[]{:S(2)}, u32[]{:S(2)}) async-start(bf16[16,464,128]{2,1,0:T(8,128)(2,1)} %broadcast_in_dim.45), calls=%async_computation | async-start | bytes 3801088 | tf_op jit(solution)/shard_map/all_to_all | solution.py:34
  29.9 0.0 copy-done.3
  29.9 0.0 copy-done.6
  30.0 5.9 %collective-permute-start = (bf16[80,512]{1,0:T(8,128)(2,1)S(1)}, bf16[80,512]{1,0:T(8,128)(2,1)S(1)}, u32[]{:S(2)}, u32[]{:S(2)}) collective-permute-start(bf16[80,512]{1,0:T(8,128)(2,1)S(1)} %fusion.4), channel_id=1, source_target_pairs={{0,0},{1,4},{2,8},{3,12},{4,16},{5,20},{6,24},{7,28},{8,1},{9,5},{... | collective-permute-start | bytes 245768 | tf_op jit(solution)/shard_map/ppermute | solution.py:582
  35.9 18.7 %collective-permute-done = bf16[80,512]{1,0:T(8,128)(2,1)S(1)} collective-permute-done((bf16[80,512]{1,0:T(8,128)(2,1)S(1)}, bf16[80,512]{1,0:T(8,128)(2,1)S(1)}, u32[]{:S(2)}, u32[]{:S(2)}) %collective-permute-start) | collective-permute-done | bytes 81952 | tf_op jit(solution)/shard_map/ppermute | solution.py:582
  54.5 3.1 %all-to-all-done.pieces = bf16[16,464,128]{2,1,0:T(8,128)(2,1)S(1)} async-done(((bf16[16,464,128]{2,1,0:T(8,128)(2,1)}), bf16[16,464,128]{2,1,0:T(8,128)(2,1)S(1)}, u32[]{:S(2)}, u32[]{:S(2)}) %all-to-all-start) | async-done | bytes 1900576 | tf_op jit(solution)/shard_map/all_to_all | solution.py:34
  57.7 0.0 copy-start.1
  57.7 1.3 broadcast_in_dim.44
  59.0 0.4 copy-done.1
  59.4 7.3 %all-to-all-start.1 = ((bf16[16,80,512]{2,1,0:T(8,128)(2,1)}), bf16[16,80,512]{2,1,0:T(8,128)(2,1)S(1)}, u32[]{:S(2)}, u32[]{:S(2)}) async-start(bf16[16,80,512]{2,1,0:T(8,128)(2,1)} %broadcast_in_dim.44), calls=%async_computation.1 | async-start | bytes 2621440 | tf_op jit(solution)/shard_map/all_to_all | solution.py:34
  66.7 0.0 reduce-scatter.5.cloned.1.call-start
  66.8 1.3 fusion
  68.1 0.0 all-gather.5.cloned.1.call-done
  68.1 13.6 %shard_map.247 = (bf16[2,4,128,384]{3,2,1,0:T(8,128)(2,1)}, f32[2,4,128,128]{3,2,1,0:T(8,128)}, bf16[2,4,128,640]{3,2,1,0:T(8,128)(2,1)}, bf16[2,4,128,512]{3,2,...) custom-call(s32[6]{0:T(128)} %stack.39.at, ...), custom_call_target="tpu_custom_call" | custom-call | flops 4194304 | bytes 8192 | tf_op jit(solution)/shard_map/pallas_call | solution.py:288
  81.7 0.0 all-gather.3.cloned.1.call-done.cot
  81.8 4.6 %shard_map.248 = (bf16[16,80,512]{2,1,0:T(8,128)(2,1)}, f32[8,1024]{1,0:T(8,128)}) custom-call(bf16[1024,640]{1,0:T(8,128)(2,1)} %bitcast.26, bf16[1024,1024]{1,0:T(8,128)(2,1)} %all-gather.3.cloned.1.call-done.cot), custom_call_target="tpu_custom_call" | custom-call | flops 2097152 | bytes 6144 | tf_op jit(solution)/shard_map/pallas_call | solution.py:507
  86.4 0.0 all-to-all-done.1.refs_1_.blocks
  86.4 0.0 copy-start
  86.4 1.1 copy-done
  87.5 4.4 %shard_map.250 = bf16[2,4,128,1024]{3,2,1,0:T(8,128)(2,1)} custom-call(bf16[2,4,128,640]{3,2,1,0:T(8,128)(2,1)} %get-tuple-element.51.both, bf16[16,80,512]{2,1,0:T(8,128)(2,1)} %copy-done, bf16[16,80,512]{2,1,0:T(8,128)(2,1)} %get-tuple-element.56.refs_13_.refs_14_.ahead), custom_call_target="tpu_custom_call" | custom-call | flops 2097152 | bytes 6144 | tf_op jit(solution)/shard_map/pallas_call | solution.py:349
  91.8 0.0 reduce-scatter.5.cloned.1.call-update
  91.9 6.7 %all-to-all-start.2 = ((bf16[16,80,512]{2,1,0:T(8,128)(2,1)}), bf16[16,80,512]{2,1,0:T(8,128)(2,1)S(1)}, u32[]{:S(2)}, u32[]{:S(2)}) async-start(bf16[16,80,512]{2,1,0:T(8,128)(2,1)} %get-tuple-element.56.refs_13_.refs_14_.ahead), calls=%async_computation.2 | async-start | bytes 2621440 | tf_op jit(solution)/shard_map/all_to_all | solution.py:34
  98.5 0.2 reduce-scatter.3.cloned.1.call-start
  98.8 16.8 %shard_map.249 = (bf16[2,4,128,1024]{3,2,1,0:T(8,128)(2,1)}, bf16[16,464,128]{2,1,0:T(8,128)(2,1)}) custom-call(s32[6]{0:T(128)} %stack.39.at, bf16[2,4,128,1024]{3,2,1,0:T(8,128)(2,1)} %bitcast.25, bf16[16,80,512]{2,1,0:T(8,128)(2,1)} %copy-done, bf16[2,4,128,384]{3,2,1,0:T(8,128)(2,1)} %get-tuple-element.47.refs_2_, ...), custom_call_target="tpu_custom_call" | custom-call | flops 6291456 | bytes 16384 | tf_op jit(solution)/shard_map/pallas_call | solution.py:478
  115.6 1.3 all-to-all-done.2
  116.9 0.0 reduce-scatter.3.cloned.1.call-update
  116.9 5.4 %all-to-all-start.3 = ((bf16[16,464,128]{2,1,0:T(8,128)(2,1)}), bf16[16,464,128]{2,1,0:T(8,128)(2,1)S(1)}, u32[]{:S(2)}, u32[]{:S(2)}) async-start(bf16[16,464,128]{2,1,0:T(8,128)(2,1)} %get-tuple-element.62), calls=%async_computation.5 | async-start | bytes 3801088 | tf_op jit(solution)/shard_map/all_to_all | solution.py:34
  122.3 0.2 reduce_sum.25
  122.5 5.6 %collective-permute-start.4 = (bf16[80,512]{1,0:T(8,128)(2,1)S(1)}, bf16[80,512]{1,0:T(8,128)(2,1)S(1)}, u32[]{:S(2)}, u32[]{:S(2)}) collective-permute-start(bf16[80,512]{1,0:T(8,128)(2,1)S(1)} %reduce_sum.25), channel_id=1, source_target_pairs={{0,0},{4,1},{8,2},{12,3},{16,4},{20,5},{24,6},{28,7},{1,8},{5,9},{... | collective-permute-start | bytes 245768 | tf_op jit(solution)/shard_map/ppermute | solution.py:603
  128.1 2.6 %collective-permute-start.5 = (bf16[80,512]{1,0:T(8,128)(2,1)S(1)}, bf16[80,512]{1,0:T(8,128)(2,1)S(1)}, u32[]{:S(2)}, u32[]{:S(2)}) collective-permute-start(bf16[80,512]{1,0:T(8,128)(2,1)S(1)} %reduce_sum.25), channel_id=1, source_target_pairs={{0,64},{4,65},{8,66},{12,67},{16,68},{20,69},{24,70},{28,71},{1,72... | collective-permute-start | bytes 245768 | tf_op jit(solution)/shard_map/ppermute | solution.py:604
  130.7 15.6 %all-to-all-done.3 = bf16[16,464,128]{2,1,0:T(8,128)(2,1)S(1)} async-done(((bf16[16,464,128]{2,1,0:T(8,128)(2,1)}), bf16[16,464,128]{2,1,0:T(8,128)(2,1)S(1)}, u32[]{:S(2)}, u32[]{:S(2)}) %all-to-all-start.3) | async-done | bytes 1900576 | tf_op jit(solution)/shard_map/all_to_all | solution.py:34
  146.3 0.3 reduce_sum.24
  146.5 3.8 %collective-permute-done.4.refs_1_ = bf16[80,512]{1,0:T(8,128)(2,1)S(1)} collective-permute-done((bf16[80,512]{1,0:T(8,128)(2,1)S(1)}, bf16[80,512]{1,0:T(8,128)(2,1)S(1)}, u32[]{:S(2)}, u32[]{:S(2)}) %collective-permute-start.4) | collective-permute-done | bytes 81952 | tf_op jit(solution)/shard_map/ppermute | solution.py:603
  150.4 0.0 copy-start.4
  150.4 3.9 %collective-permute-done.5.refs_2_ = bf16[80,512]{1,0:T(8,128)(2,1)S(1)} collective-permute-done((bf16[80,512]{1,0:T(8,128)(2,1)S(1)}, bf16[80,512]{1,0:T(8,128)(2,1)S(1)}, u32[]{:S(2)}, u32[]{:S(2)}) %collective-permute-start.5) | collective-permute-done | bytes 81952 | tf_op jit(solution)/shard_map/ppermute | solution.py:604
  154.2 0.0 copy-start.5
  154.3 0.7 maximum_maximum_fusion
  155.0 5.5 %all-to-all-start.4 = ((bf16[8,128,128]{2,1,0:T(8,128)(2,1)}), bf16[8,128,128]{2,1,0:T(8,128)(2,1)S(1)}, u32[]{:S(2)}, u32[]{:S(2)}) async-start(bf16[8,128,128]{2,1,0:T(8,128)(2,1)} %maximum_maximum_fusion), calls=%async_computation.6 | async-start | bytes 524288 | tf_op jit(solution)/shard_map/all_to_all | solution.py:34
  160.5 8.3 %reduce-scatter.3.cloned.1.call-done.norm_grad = bf16[128,1024]{1,0:T(8,128)(2,1)} async-done(((bf16[1024,1024]{1,0:T(8,128)(2,1)}), bf16[128,1024]{1,0:T(8,128)(2,1)}) %reduce-scatter.3.cloned.1.call-update) | async-done | bytes 262160 | tf_op jit(solution)/shard_map/reduce_scatter | solution.py:537
  168.7 3.2 %shard_map.251 = (bf16[128,1024]{1,0:T(8,128)(2,1)}, f32[128,1024]{1,0:T(8,128)}) custom-call(s32[6]{0:T(128)} %stack.39.at, bf16[128,1024]{1,0:T(8,128)(2,1)} %tokens.3, bf16[128,1024]{1,0:T(8,128)(2,1)} %out_grad.1, bf16[128,1024]{1,0:T(8,128)(2,1)} %reduce-scatter.3.cloned.1.call-done.norm_grad, ...), custom_call_target="tpu_custom_call" | custom-call | bytes 1024 | tf_op jit(solution)/shard_map/pallas_call | solution.py:50
  171.9 0.0 copy-done.4
  171.9 0.0 copy-done.5
  172.0 0.0 all-to-all-done.4.refs_0_
  172.0 0.0 copy-start.2
  172.0 0.7 copy-done.2
  172.7 2.0 %shard_map.252 = (f32[16,3072]{1,0:T(8,128)}, f32[16,4096]{1,0:T(8,128)}, f32[16]{0:T(128)}, f32[16]{0:T(128)}, f32[16]{0:T(128)}, /*index=5*/f32[16]{0:T(128)},...) custom-call(s32[6]{0:T(128)} %stack.39.at, ...), custom_call_target="tpu_custom_call" | custom-call | bytes 1024 | tf_op jit(solution)/shard_map/pallas_call | solution.py:50
  (11 shorter events, 0.1 us)
Async XLA Ops:
  7.2 60.9 %all-gather.5.cloned.1.call-start = ((), (), s32[]{:S(2)}) async-start(), calls=%async_computation.8 | async-start | bytes 2359296 | tf_op jit(solution)/shard_map/all_gather | solution.py:533
  12.4 69.3 %all-gather.3.cloned.1.call-start = ((), (), s32[]{:S(2)}) async-start(), calls=%async_computation.7 | async-start | bytes 2359296 | tf_op jit(solution)/shard_map/all_gather | solution.py:533
  14.0 3.5 %collective-permute-start.2 = (bf16[128,128]{1,0:T(8,128)(2,1)S(1)}, bf16[128,128]{1,0:T(8,128)(2,1)S(1)}, u32[]{:S(2)}, u32[]{:S(2)}) collective-permute-start(bf16[128,128]{1,0:T(8,128)(2,1)S(1)} %get-tuple-element.78), channel_id=1, source_target_pairs={{0,32},{1,33},{32,0},{33,1},{2,34},{3,35},{34,2},{35,3},{4,36},{5,... | collective-permute-start | bytes 98312 | tf_op jit(solution)/shard_map/ppermute | solution.py:30
  16.2 3.7 %collective-permute-start.3 = (bf16[128,128]{1,0:T(8,128)(2,1)S(1)}, bf16[128,128]{1,0:T(8,128)(2,1)S(1)}, u32[]{:S(2)}, u32[]{:S(2)}) collective-permute-start(bf16[128,128]{1,0:T(8,128)(2,1)S(1)} %get-tuple-element.77), channel_id=1, source_target_pairs={{0,33},{1,32},{32,1},{33,0},{2,35},{3,34},{34,3},{35,2},{4,37},{5,... | collective-permute-start | bytes 98312 | tf_op jit(solution)/shard_map/ppermute | solution.py:30
  17.2 2.8 %collective-permute-start.1 = (bf16[128,128]{1,0:T(8,128)(2,1)S(1)}, bf16[128,128]{1,0:T(8,128)(2,1)S(1)}, u32[]{:S(2)}, u32[]{:S(2)}) collective-permute-start(bf16[128,128]{1,0:T(8,128)(2,1)S(1)} %get-tuple-element.79), channel_id=1, source_target_pairs={{0,1},{1,0},{32,33},{33,32},{2,3},{3,2},{34,35},{35,34},{4,5},{5,4... | collective-permute-start | bytes 98312 | tf_op jit(solution)/shard_map/ppermute | solution.py:30
  22.2 7.7 %copy-start.3 = (bf16[64,1024]{1,0:T(8,128)(2,1)S(1)}, bf16[64,1024]{1,0:T(8,128)(2,1)}, u32[]{:S(2)}) copy-start(bf16[64,1024]{1,0:T(8,128)(2,1)} %param.25) | copy-start | bytes 393220
  22.2 7.8 %copy-start.6 = (bf16[16,1024]{1,0:T(8,128)(2,1)S(1)}, bf16[16,1024]{1,0:T(8,128)(2,1)}, u32[]{:S(2)}) copy-start(bf16[16,1024]{1,0:T(8,128)(2,1)} %param.21) | copy-start | bytes 98308
  22.2 35.5 %all-to-all-start = ((bf16[16,464,128]{2,1,0:T(8,128)(2,1)}), bf16[16,464,128]{2,1,0:T(8,128)(2,1)S(1)}, u32[]{:S(2)}, u32[]{:S(2)}) async-start(bf16[16,464,128]{2,1,0:T(8,128)(2,1)} %broadcast_in_dim.45), calls=%async_computation | async-start | bytes 3801088 | tf_op jit(solution)/shard_map/all_to_all | solution.py:34
  30.0 24.6 %collective-permute-start = (bf16[80,512]{1,0:T(8,128)(2,1)S(1)}, bf16[80,512]{1,0:T(8,128)(2,1)S(1)}, u32[]{:S(2)}, u32[]{:S(2)}) collective-permute-start(bf16[80,512]{1,0:T(8,128)(2,1)S(1)} %fusion.4), channel_id=1, source_target_pairs={{0,0},{1,4},{2,8},{3,12},{4,16},{5,20},{6,24},{7,28},{8,1},{9,5},{... | collective-permute-start | bytes 245768 | tf_op jit(solution)/shard_map/ppermute | solution.py:582
  57.7 1.7 copy-start.1
  59.4 27.0 %all-to-all-start.1 = ((bf16[16,80,512]{2,1,0:T(8,128)(2,1)}), bf16[16,80,512]{2,1,0:T(8,128)(2,1)S(1)}, u32[]{:S(2)}, u32[]{:S(2)}) async-start(bf16[16,80,512]{2,1,0:T(8,128)(2,1)} %broadcast_in_dim.44), calls=%async_computation.1 | async-start | bytes 2621440 | tf_op jit(solution)/shard_map/all_to_all | solution.py:34
  66.7 87.5 %reduce-scatter.5.cloned.1.call-start = ((), (), s32[]{:S(2)}) async-start(), calls=%async_computation.10 | async-start | bytes 2359296 | tf_op jit(solution)/shard_map/reduce_scatter | solution.py:537
  86.4 1.1 copy-start
  91.9 25.0 %all-to-all-start.2 = ((bf16[16,80,512]{2,1,0:T(8,128)(2,1)}), bf16[16,80,512]{2,1,0:T(8,128)(2,1)S(1)}, u32[]{:S(2)}, u32[]{:S(2)}) async-start(bf16[16,80,512]{2,1,0:T(8,128)(2,1)} %get-tuple-element.56.refs_13_.refs_14_.ahead), calls=%async_computation.2 | async-start | bytes 2621440 | tf_op jit(solution)/shard_map/all_to_all | solution.py:34
  98.5 70.2 %reduce-scatter.3.cloned.1.call-start = ((), (), s32[]{:S(2)}) async-start(), calls=%async_computation.9 | async-start | bytes 2359296 | tf_op jit(solution)/shard_map/reduce_scatter | solution.py:537
  116.9 29.4 %all-to-all-start.3 = ((bf16[16,464,128]{2,1,0:T(8,128)(2,1)}), bf16[16,464,128]{2,1,0:T(8,128)(2,1)S(1)}, u32[]{:S(2)}, u32[]{:S(2)}) async-start(bf16[16,464,128]{2,1,0:T(8,128)(2,1)} %get-tuple-element.62), calls=%async_computation.5 | async-start | bytes 3801088 | tf_op jit(solution)/shard_map/all_to_all | solution.py:34
  122.5 27.8 %collective-permute-start.4 = (bf16[80,512]{1,0:T(8,128)(2,1)S(1)}, bf16[80,512]{1,0:T(8,128)(2,1)S(1)}, u32[]{:S(2)}, u32[]{:S(2)}) collective-permute-start(bf16[80,512]{1,0:T(8,128)(2,1)S(1)} %reduce_sum.25), channel_id=1, source_target_pairs={{0,0},{4,1},{8,2},{12,3},{16,4},{20,5},{24,6},{28,7},{1,8},{5,9},{... | collective-permute-start | bytes 245768 | tf_op jit(solution)/shard_map/ppermute | solution.py:603
  128.1 26.1 %collective-permute-start.5 = (bf16[80,512]{1,0:T(8,128)(2,1)S(1)}, bf16[80,512]{1,0:T(8,128)(2,1)S(1)}, u32[]{:S(2)}, u32[]{:S(2)}) collective-permute-start(bf16[80,512]{1,0:T(8,128)(2,1)S(1)} %reduce_sum.25), channel_id=1, source_target_pairs={{0,64},{4,65},{8,66},{12,67},{16,68},{20,69},{24,70},{28,71},{1,72... | collective-permute-start | bytes 245768 | tf_op jit(solution)/shard_map/ppermute | solution.py:604
  150.4 21.6 %copy-start.4 = (bf16[80,512]{1,0:T(8,128)(2,1)}, bf16[80,512]{1,0:T(8,128)(2,1)S(1)}, u32[]{:S(2)}) copy-start(bf16[80,512]{1,0:T(8,128)(2,1)S(1)} %collective-permute-done.4.refs_1_) | copy-start | bytes 245764
  154.2 17.7 %copy-start.5 = (bf16[80,512]{1,0:T(8,128)(2,1)}, bf16[80,512]{1,0:T(8,128)(2,1)S(1)}, u32[]{:S(2)}) copy-start(bf16[80,512]{1,0:T(8,128)(2,1)S(1)} %collective-permute-done.5.refs_2_) | copy-start | bytes 245764
  155.0 17.0 %all-to-all-start.4 = ((bf16[8,128,128]{2,1,0:T(8,128)(2,1)}), bf16[8,128,128]{2,1,0:T(8,128)(2,1)S(1)}, u32[]{:S(2)}, u32[]{:S(2)}) async-start(bf16[8,128,128]{2,1,0:T(8,128)(2,1)} %maximum_maximum_fusion), calls=%async_computation.6 | async-start | bytes 524288 | tf_op jit(solution)/shard_map/all_to_all | solution.py:34
  172.0 0.7 copy-start.2
Sparse Core Ops, SparseCore 0:
  12.6 28.7 all-gather.4
  43.1 25.4 all-gather.2
  92.0 32.4 reduce-scatter.4
  126.7 41.9 reduce-scatter.2
